TPU v7x, 128 devices: a whole 4x4x4 slice. The times are simulated.
128 devices in a mesh: prop: 16 (over z, x_hi, core), cross: 8 (over x_lo, y).
Axes of the slice: x: 4 (x_hi: 2, x_lo: 2; x = x_hi * 2 + x_lo), y: 4, z: 4, core: 2. Of those that a mesh axis runs over, the one named last changes fastest.
Arguments:
- gas: float32 [5, 64, 256, 512], P(None, 'prop', 'cross'), may hold values from -4 to 4
- parcel_state: float32 [2, 2097152], P(None, ('prop', 'cross')), may hold values from 0.5 to 2
- parcel_cell: int32 [2097152], P(('prop', 'cross')), may hold values from 0 to 65535
- parcel_dest: int32 [2097152], P(('prop', 'cross')), may hold values from 0 to 65535
- send_slot: int32 [2097152], P(('prop', 'cross')), may hold values from -1 to 4095, as said below
- face_counts: int32 [16, 8, 2], P('prop', 'cross'), may hold values from 0 to 2048, as said below
Outputs:
- gas_out: float32 [5, 64, 256, 512], P(None, 'prop', 'cross')
- parcels_out: float32 [2, 2097152], P(None, ('prop', 'cross'))
- arrivals: float32 [2, 3, 262144], P(None, None, ('prop', 'cross'))
Inputs may be any that keep to these rules, and one draw needn't show every extreme that they name: face_counts[p, c, 0] and face_counts[p, c, 1] count the parcels that device (p, c) sends toward lower and higher propagation index; the devices of at most three adjacent slabs send 2048 through both faces, which is reached in every draw. `send_slot`: -1 for a parcel that stays; otherwise f * 2048 + j with face f (0 lower, 1 higher) and j below that device's face_counts for f; on each device every such code is used by exactly one parcel.
All inputs are finite; a program needn't handle non-finite values.
Results may differ from a plain program's by a relative error of at most 0.0003.
Values sent between devices are 32-bit elements; how exact they have to be, the bound alone decides.
A program may use at most 64 MiB of HBM per device.

v0:
```python
import jax
import jax.numpy as jnp
from jax import lax
from jax.sharding import PartitionSpec as P

SUBSTEPS = 2


def padded_2(x, sides, width):
    for axis, dim in sides:
        devices, length = (lax.axis_size(axis), x.shape[dim])
        up = [(i, (i + 1) % devices) for i in range(devices - 1)]
        down = [(j, i) for i, j in up]
        last = lax.slice_in_dim(x, length - width, length, axis=dim)
        initial = lax.slice_in_dim(x, 0, width, axis=dim)
        before = lax.ppermute(last, axis, up)
        after = lax.ppermute(initial, axis, down)
        x = jnp.concatenate([before, x, after], axis=dim)
    return x


def shifted(block, axis, distance):
    devices = range(lax.axis_size(axis))
    route = [(i - distance, i) for i in devices if i - distance in devices]
    return lax.ppermute(block, axis, route)


def advance(padded):
    zpad = jnp.pad(padded, ((0, 0), (0, 0), (0, 0), (1, 1)))
    center = zpad[:, 1:-1, 1:-1, 1:-1]
    xplus = zpad[:, 2:, 1:-1, 1:-1]
    xminus = zpad[:, :-2, 1:-1, 1:-1]
    yplus = zpad[:, 1:-1, 2:, 1:-1]
    yminus = zpad[:, 1:-1, :-2, 1:-1]
    zplus = zpad[:, 1:-1, 1:-1, 2:]
    zminus = zpad[:, 1:-1, 1:-1, :-2]
    carry_x = center[0:1]
    carry_y = center[1:2]
    carry_z = center[2:3]
    advect = 0.5 * (
        carry_x * (xplus - xminus) + carry_y * (yplus - yminus) + carry_z * (zplus - zminus)
    )
    laplace = xplus + xminus + yplus + yminus + zplus + zminus - 6.0 * center
    fresh = center - 0.1 * advect + 0.12 * laplace
    return fresh.at[2].add(0.1 * center[3])


def burn(state, seen):
    mass = state[0]
    temper = state[1]
    hot = temper + 0.3 * (seen - temper)
    burned = 0.2 * mass * (1.0 + 0.5 * jnp.tanh(hot))
    return jnp.stack([mass - burned, hot + 0.5 * burned, burned], axis=0)


def on_device(gas, parcel_state, parcel_cell, parcel_dest, send_slot, face_counts):
    rows = gas.shape[1]
    cols = gas.shape[2]
    depth = gas.shape[3]
    settled = gas
    for step in range(SUBSTEPS):
        padded = padded_2(settled, (("prop", 1), ("cross", 2)), 1)
        settled = advance(padded)
    ncell = rows * cols * depth
    seen = settled[3].reshape(ncell)[parcel_cell]
    records = burn(parcel_state, seen)
    parcels = parcel_state.shape[1]
    slots = parcels // 8
    index = jnp.where(send_slot >= 0, send_slot, 2 * slots)
    rec_buf = jnp.zeros((3, 2 * slots + 1), jnp.float32).at[:, index].set(records)[:, : 2 * slots]
    rec_buf = rec_buf.reshape(3, 2, slots).transpose(1, 0, 2)
    dest_buf = (
        jnp.zeros((2 * slots + 1,), jnp.int32)
        .at[index]
        .set(parcel_dest)[: 2 * slots]
        .reshape(2, slots)
    )
    counts = face_counts.reshape(2)
    live = jnp.arange(slots, dtype=jnp.int32)[None, :] < counts[:, None]
    rec_buf = jnp.where(live[:, None, :], rec_buf, jnp.zeros_like(rec_buf))
    dest_buf = jnp.where(live, dest_buf, jnp.zeros_like(dest_buf))
    below_rec, below_dest = shifted((rec_buf[1], dest_buf[1]), "prop", 1)
    above_rec, above_dest = shifted((rec_buf[0], dest_buf[0]), "prop", -1)
    stay = send_slot < 0
    release = (
        jnp.zeros((ncell,), jnp.float32)
        .at[parcel_dest]
        .add(jnp.where(stay, records[2], jnp.zeros_like(records[2])))
    )
    arrived_cells = jnp.concatenate([below_dest, above_dest], axis=0)
    arrived_burn = jnp.concatenate([below_rec[2], above_rec[2]], axis=0)
    release = release.at[arrived_cells].add(arrived_burn)
    release = release.reshape(rows, cols, depth)
    gas_out = jnp.concatenate(
        [settled[:3], (settled[3] + 1.5 * release)[None], (settled[4] + release)[None]], axis=0
    )
    arrivals = jnp.stack([below_rec, above_rec], axis=0)
    return (gas_out, records[:2], arrivals)


def solution(mesh):
    in_specs = (
        P(None, "prop", "cross", None),
        P(None, ("prop", "cross")),
        P(("prop", "cross")),
        P(("prop", "cross")),
        P(("prop", "cross")),
        P("prop", "cross", None),
    )
    out_specs = (
        P(None, "prop", "cross", None),
        P(None, ("prop", "cross")),
        P(None, None, ("prop", "cross")),
    )
    return jax.shard_map(
        on_device, mesh=mesh, in_specs=in_specs, out_specs=out_specs, check_vma=False
    )
```

profile of v0, /device:TPU:7, one launch (start us, length us, event | category | flops | bytes accessed | tf_op | source)
XLA Modules:
  0.0 388.5 jit_solution(10218259018690716112)
XLA Ops:
  0.6 0.0 copy-start
  0.6 0.0 copy-start.5
  0.7 1.2 fusion.14
  1.9 4.9 %collective-permute-start.1 = (f32[5,1,32,512]{3,2,1,0:T(8,128)S(1)}, f32[5,1,32,512]{3,2,1,0:T(8,128)S(1)}, u32[]{:S(2)}, u32[]{:S(2)}) collective-permute-start(f32[5,1,32,512]{3,2,1,0:T(8,128)S(1)} %get-tuple-element.48), channel_id=1, source_target_pairs={{0,8},{8,16},{16,24},{24,32},{32,40},{40,48},{48,56},{56,64},{64,7... | collective-permute-start | bytes 983048 | tf_op jit(solution)/shard_map/ppermute | solution.py:16
  6.9 1.9 collective-permute-start
  8.8 0.9 compare_select_fusion
  9.7 60.4 %scatter_custom_fusion.1 = s32[4097]{0:T(1024)S(1)} fusion(s32[16384]{0:T(1024)S(1)} %compare_select_fusion, s32[16384]{0:T(1024)S(1)} %copy-done.5, s32[]{:T(128)} %constant.79.clone.1), kind=kCustom, calls=%fused_computation.69 | custom fusion | bytes 16392 | tf_op jit(solution)/shard_map/scatter | solution.py:75
  70.1 0.1 broadcast_select_fusion
  70.2 6.0 %collective-permute-start.8 = (s32[2048]{0:T(1024)S(1)}, s32[2048]{0:T(1024)S(1)}, u32[]{:S(2)}, u32[]{:S(2)}) collective-permute-start(s32[2048]{0:T(1024)S(1)} %bitcast.50), channel_id=1, source_target_pairs={{0,8},{8,16},{16,24},{24,32},{32,40},{40,48},{48,56},{56,64},{64,7... | collective-permute-start | bytes 24584 | tf_op jit(solution)/shard_map/ppermute | solution.py:25
  76.2 1.9 collective-permute-start.9
  78.2 0.6 compare_select_fusion.3
  78.8 0.1 iota_compare_fusion.2
  78.9 0.0 collective-permute-done.1
  79.0 0.1 constant_dynamic-update-slice_fusion.1
  79.1 0.0 collective-permute-done
  79.1 0.1 fusion.12
  79.2 4.0 %collective-permute-start.2 = (f32[5,6,1,512]{3,2,1,0:T(1,128)S(1)}, f32[5,6,1,512]{3,2,1,0:T(1,128)S(1)}, u32[]{:S(2)}, u32[]{:S(2)}) collective-permute-start(f32[5,6,1,512]{3,2,1,0:T(1,128)S(1)} %get-tuple-element.37), channel_id=1, source_target_pairs={{1,0},{2,1},{3,2},{4,3},{5,4},{6,5},{7,6},{9,8},{10,9},{11,10},{12... | collective-permute-start | bytes 184328 | tf_op jit(solution)/shard_map/ppermute | solution.py:17
  83.3 1.9 collective-permute-start.3
  85.2 0.1 slice_bitcast_fusion.4
  85.3 0.0 collective-permute-done.2
  85.3 5.1 %collective-permute-done.3 = f32[5,6,1,512]{3,2,1,0:T(1,128)S(1)} collective-permute-done((f32[5,6,1,512]{3,2,1,0:T(1,128)S(1)}, f32[5,6,1,512]{3,2,1,0:T(1,128)S(1)}, u32[]{:S(2)}, u32[]{:S(2)}) %collective-permute-start.3) | collective-permute-done | bytes 61472 | tf_op jit(solution)/shard_map/ppermute | solution.py:16
  90.3 1.4 select_maximum_fusion.4
  91.7 1.5 multiply_add_fusion.1
  93.2 0.1 fusion.7
  93.4 4.2 %collective-permute-start.4 = (f32[5,1,32,512]{3,2,1,0:T(8,128)S(1)}, f32[5,1,32,512]{3,2,1,0:T(8,128)S(1)}, u32[]{:S(2)}, u32[]{:S(2)}) collective-permute-start(f32[5,1,32,512]{3,2,1,0:T(8,128)S(1)} %get-tuple-element.43), channel_id=1, source_target_pairs={{8,0},{16,8},{24,16},{32,24},{40,32},{48,40},{56,48},{64,56},{72,6... | collective-permute-start | bytes 983048 | tf_op jit(solution)/shard_map/ppermute | solution.py:17
  97.6 5.8 %collective-permute-start.5 = (f32[5,1,32,512]{3,2,1,0:T(8,128)S(1)}, f32[5,1,32,512]{3,2,1,0:T(8,128)S(1)}, u32[]{:S(2)}, u32[]{:S(2)}) collective-permute-start(f32[5,1,32,512]{3,2,1,0:T(8,128)S(1)} %get-tuple-element.42), channel_id=1, source_target_pairs={{0,8},{8,16},{16,24},{24,32},{32,40},{40,48},{48,56},{56,64},{64,7... | collective-permute-start | bytes 983048 | tf_op jit(solution)/shard_map/ppermute | solution.py:16
  103.4 0.0 collective-permute-done.8
  103.4 0.0 collective-permute-done.9
  103.5 0.6 compare_select_fusion.4
  104.1 3.7 collective-permute-done.4
  107.7 0.0 collective-permute-done.5
  107.7 0.1 pad_maximum_fusion.15
  107.8 1.9 collective-permute-start.6
  109.8 3.4 collective-permute-start.7
  113.2 0.0 collective-permute-done.6
  113.2 3.6 collective-permute-done.7
  116.8 1.4 select_maximum_fusion
  118.3 1.7 multiply_add_fusion
  120.0 0.1 fusion.4
  120.1 0.1 copy.15
  120.2 0.0 copy-start.1
  120.2 90.5 %gather_fusion = f32[16384]{0:T(1024)S(1)} fusion(f32[65536]{0:T(1024)S(1)} %bitcast.36, s32[16384]{0:T(1024)S(1)} %fusion.9), kind=kCustom, calls=%fused_computation | custom fusion | bytes 196608 | tf_op jit(solution)/shard_map/gather | solution.py:65
  210.7 0.0 copy-done.1
  210.7 0.2 slice_subtract_fusion
  210.9 0.8 multiply_add_fusion.3
  211.8 0.2 maximum_bitcast_fusion
  212.0 0.8 pad_maximum_fusion.13
  212.7 5.0 %copy.12 = f32[16384,3]{1,0:T(8,128)} copy(f32[16384,3]{0,1:T(4,128)S(1)} %maximum_bitcast_fusion) | data formatting | bytes 393216 | tf_op jit(solution)/shard_map/stack | solution.py:53
  217.8 41.4 %scatter_custom_fusion.2 = f32[3,4097]{0,1:T(8,128)S(1)} fusion(s32[16384]{0:T(1024)} %copy-done.7, f32[16384,3]{1,0:T(8,128)} %copy.12, f32[]{:T(128)} %constant.73.clone.1), kind=kCustom, calls=%fused_computation.29 | custom fusion | bytes 49676 | tf_op jit(solution)/shard_map/scatter | solution.py:70
  259.1 1.5 slice.270
  260.6 2.2 copy.13
  262.9 7.6 %collective-permute-start.10 = (f32[3,2048]{1,0:T(4,128)S(1)}, f32[3,2048]{1,0:T(4,128)S(1)}, u32[]{:S(2)}, u32[]{:S(2)}) collective-permute-start(f32[3,2048]{1,0:T(4,128)S(1)} %get-tuple-element.52), channel_id=1, source_target_pairs={{0,8},{8,16},{16,24},{24,32},{32,40},{40,48},{48,56},{56,64},{64,7... | collective-permute-start | bytes 73736 | tf_op jit(solution)/shard_map/ppermute | solution.py:25
  270.6 1.9 collective-permute-start.11
  272.5 0.0 copy-done.2
  272.5 0.0 copy-done.3
  272.6 0.1 slice.265
  272.6 86.1 %scatter_custom_fusion = f32[65536]{0:T(1024)S(1)} fusion(s32[16384]{0:T(1024)} %compare_select_fusion.3, f32[16384]{0:T(1024)S(1)} %multiply_select_fusion, f32[]{:T(128)} %constant.73.clone.1), kind=kCustom, calls=%fused_computation.48 | custom fusion | flops 16384 | bytes 262656 | tf_op jit(solution)/shard_map/scatter-add | solution.py:88
  358.7 0.0 collective-permute-done.10
  358.7 0.0 collective-permute-done.11
  358.8 0.7 copy.14
  359.5 0.0 copy-done.4
  359.5 27.7 %scatter_fusion = f32[65536]{0:T(1024)S(1)} fusion(f32[65536]{0:T(1024)S(1)} %scatter_custom_fusion, s32[4096]{0:T(1024)S(1)} %bitcast.43, f32[4096]{0:T(1024)S(1)} %pad_maximum_fusion.18), kind=kCustom, calls=%fused_computation.4 | custom fusion | flops 4096 | bytes 65536 | tf_op jit(solution)/shard_map/scatter-add | solution.py:92
  387.3 0.1 multiply_add_fusion.2
  387.3 1.2 pad_maximum_fusion.12
  (28 shorter events, 0.4 us)
Async XLA Ops:
  0.6 78.3 %copy-start = (f32[5,4,32,512]{3,2,1,0:T(8,128)S(1)}, f32[5,4,32,512]{3,2,1,0:T(8,128)}, u32[]{:S(2)}) copy-start(f32[5,4,32,512]{3,2,1,0:T(8,128)} %param.10) | copy-start | bytes 3932164
  0.6 9.0 %copy-start.5 = (s32[16384]{0:T(1024)S(1)}, s32[16384]{0:T(1024)}, u32[]{:S(2)}) copy-start(s32[16384]{0:T(1024)} %param.13) | copy-start | bytes 196612
  0.7 69.4 %copy-start.8 = (s32[1,1,2]{2,1,0:T(1,128)S(1)}, s32[1,1,2]{2,1,0:T(1,128)}, u32[]{:S(2)}) copy-start(s32[1,1,2]{2,1,0:T(1,128)} %param.15) | copy-start | bytes 28
  0.7 78.1 %copy-start.6 = (s32[16384]{0:T(1024)S(1)}, s32[16384]{0:T(1024)}, u32[]{:S(2)}) copy-start(s32[16384]{0:T(1024)} %param.12) | copy-start | bytes 196612
  1.9 77.0 %collective-permute-start.1 = (f32[5,1,32,512]{3,2,1,0:T(8,128)S(1)}, f32[5,1,32,512]{3,2,1,0:T(8,128)S(1)}, u32[]{:S(2)}, u32[]{:S(2)}) collective-permute-start(f32[5,1,32,512]{3,2,1,0:T(8,128)S(1)} %get-tuple-element.48), channel_id=1, source_target_pairs={{0,8},{8,16},{16,24},{24,32},{32,40},{40,48},{48,56},{56,64},{64,7... | collective-permute-start | bytes 983048 | tf_op jit(solution)/shard_map/ppermute | solution.py:16
  6.9 72.2 %collective-permute-start = (f32[5,1,32,512]{3,2,1,0:T(8,128)S(1)}, f32[5,1,32,512]{3,2,1,0:T(8,128)S(1)}, u32[]{:S(2)}, u32[]{:S(2)}) collective-permute-start(f32[5,1,32,512]{3,2,1,0:T(8,128)S(1)} %get-tuple-element.47), channel_id=1, source_target_pairs={{8,0},{16,8},{24,16},{32,24},{40,32},{48,40},{56,48},{64,56},{72,6... | collective-permute-start | bytes 983048 | tf_op jit(solution)/shard_map/ppermute | solution.py:17
  9.7 82.1 %copy-start.7 = (s32[16384]{0:T(1024)}, s32[16384]{0:T(1024)S(1)}, u32[]{:S(2)}) copy-start(s32[16384]{0:T(1024)S(1)} %compare_select_fusion) | copy-start | bytes 196612
  70.2 33.3 %collective-permute-start.8 = (s32[2048]{0:T(1024)S(1)}, s32[2048]{0:T(1024)S(1)}, u32[]{:S(2)}, u32[]{:S(2)}) collective-permute-start(s32[2048]{0:T(1024)S(1)} %bitcast.50), channel_id=1, source_target_pairs={{0,8},{8,16},{16,24},{24,32},{32,40},{40,48},{48,56},{56,64},{64,7... | collective-permute-start | bytes 24584 | tf_op jit(solution)/shard_map/ppermute | solution.py:25
  76.2 27.2 %collective-permute-start.9 = (s32[2048]{0:T(1024)S(1)}, s32[2048]{0:T(1024)S(1)}, u32[]{:S(2)}, u32[]{:S(2)}) collective-permute-start(s32[2048]{0:T(1024)S(1)} %bitcast.48), channel_id=1, source_target_pairs={{8,0},{16,8},{24,16},{32,24},{40,32},{48,40},{56,48},{64,56},{72,6... | collective-permute-start | bytes 24584 | tf_op jit(solution)/shard_map/ppermute | solution.py:25
  79.2 6.0 %collective-permute-start.2 = (f32[5,6,1,512]{3,2,1,0:T(1,128)S(1)}, f32[5,6,1,512]{3,2,1,0:T(1,128)S(1)}, u32[]{:S(2)}, u32[]{:S(2)}) collective-permute-start(f32[5,6,1,512]{3,2,1,0:T(1,128)S(1)} %get-tuple-element.37), channel_id=1, source_target_pairs={{1,0},{2,1},{3,2},{4,3},{5,4},{6,5},{7,6},{9,8},{10,9},{11,10},{12... | collective-permute-start | bytes 184328 | tf_op jit(solution)/shard_map/ppermute | solution.py:17
  83.3 7.1 %collective-permute-start.3 = (f32[5,6,1,512]{3,2,1,0:T(1,128)S(1)}, f32[5,6,1,512]{3,2,1,0:T(1,128)S(1)}, u32[]{:S(2)}, u32[]{:S(2)}) collective-permute-start(f32[5,6,1,512]{3,2,1,0:T(1,128)S(1)} %get-tuple-element.36), channel_id=1, source_target_pairs={{0,1},{1,2},{2,3},{3,4},{4,5},{5,6},{6,7},{8,9},{9,10},{10,11},{11... | collective-permute-start | bytes 184328 | tf_op jit(solution)/shard_map/ppermute | solution.py:16
  93.4 14.3 %collective-permute-start.4 = (f32[5,1,32,512]{3,2,1,0:T(8,128)S(1)}, f32[5,1,32,512]{3,2,1,0:T(8,128)S(1)}, u32[]{:S(2)}, u32[]{:S(2)}) collective-permute-start(f32[5,1,32,512]{3,2,1,0:T(8,128)S(1)} %get-tuple-element.43), channel_id=1, source_target_pairs={{8,0},{16,8},{24,16},{32,24},{40,32},{48,40},{56,48},{64,56},{72,6... | collective-permute-start | bytes 983048 | tf_op jit(solution)/shard_map/ppermute | solution.py:17
  97.6 10.1 %collective-permute-start.5 = (f32[5,1,32,512]{3,2,1,0:T(8,128)S(1)}, f32[5,1,32,512]{3,2,1,0:T(8,128)S(1)}, u32[]{:S(2)}, u32[]{:S(2)}) collective-permute-start(f32[5,1,32,512]{3,2,1,0:T(8,128)S(1)} %get-tuple-element.42), channel_id=1, source_target_pairs={{0,8},{8,16},{16,24},{24,32},{32,40},{40,48},{48,56},{56,64},{64,7... | collective-permute-start | bytes 983048 | tf_op jit(solution)/shard_map/ppermute | solution.py:16
  107.8 5.4 %collective-permute-start.6 = (f32[5,6,1,512]{3,2,1,0:T(1,128)S(1)}, f32[5,6,1,512]{3,2,1,0:T(1,128)S(1)}, u32[]{:S(2)}, u32[]{:S(2)}) collective-permute-start(f32[5,6,1,512]{3,2,1,0:T(1,128)S(1)} %get-tuple-element.35), channel_id=1, source_target_pairs={{1,0},{2,1},{3,2},{4,3},{5,4},{6,5},{7,6},{9,8},{10,9},{11,10},{12... | collective-permute-start | bytes 184328 | tf_op jit(solution)/shard_map/ppermute | solution.py:17
  109.8 7.1 %collective-permute-start.7 = (f32[5,6,1,512]{3,2,1,0:T(1,128)S(1)}, f32[5,6,1,512]{3,2,1,0:T(1,128)S(1)}, u32[]{:S(2)}, u32[]{:S(2)}) collective-permute-start(f32[5,6,1,512]{3,2,1,0:T(1,128)S(1)} %get-tuple-element.34), channel_id=1, source_target_pairs={{0,1},{1,2},{2,3},{3,4},{4,5},{5,6},{6,7},{8,9},{9,10},{10,11},{11... | collective-permute-start | bytes 184328 | tf_op jit(solution)/shard_map/ppermute | solution.py:16
  120.2 90.6 %copy-start.1 = (f32[2,16384]{1,0:T(2,128)S(1)}, f32[2,16384]{1,0:T(2,128)}, u32[]{:S(2)}) copy-start(f32[2,16384]{1,0:T(2,128)} %param.11) | copy-start | bytes 393220
  260.6 11.9 %copy-start.2 = (f32[1,16384]{1,0:T(1,128)S(1)}, f32[1,16384]{1,0:T(1,128)}, u32[]{:S(2)}) copy-start(f32[1,16384]{1,0:T(1,128)} %get-tuple-element.51) | copy-start | bytes 196612
  260.6 11.9 %copy-start.3 = (s32[16384]{0:T(1024)S(1)}, s32[16384]{0:T(1024)}, u32[]{:S(2)}) copy-start(s32[16384]{0:T(1024)} %param.14) | copy-start | bytes 196612
  262.9 96.6 %copy-start.4 = (s32[4096,1]{0,1:T(1,128)S(1)}, s32[4096,1]{0,1:T(1,128)}, u32[]{:S(2)}) copy-start(s32[4096,1]{0,1:T(1,128)} %compare_select_fusion.4) | copy-start | bytes 49156
  262.9 95.8 %collective-permute-start.10 = (f32[3,2048]{1,0:T(4,128)S(1)}, f32[3,2048]{1,0:T(4,128)S(1)}, u32[]{:S(2)}, u32[]{:S(2)}) collective-permute-start(f32[3,2048]{1,0:T(4,128)S(1)} %get-tuple-element.52), channel_id=1, source_target_pairs={{0,8},{8,16},{16,24},{24,32},{32,40},{40,48},{48,56},{56,64},{64,7... | collective-permute-start | bytes 73736 | tf_op jit(solution)/shard_map/ppermute | solution.py:25
  270.6 88.2 %collective-permute-start.11 = (f32[3,2048]{1,0:T(4,128)S(1)}, f32[3,2048]{1,0:T(4,128)S(1)}, u32[]{:S(2)}, u32[]{:S(2)}) collective-permute-start(f32[3,2048]{1,0:T(4,128)S(1)} %get-tuple-element.53), channel_id=1, source_target_pairs={{8,0},{16,8},{24,16},{32,24},{40,32},{48,40},{56,48},{64,56},{72,6... | collective-permute-start | bytes 73736 | tf_op jit(solution)/shard_map/ppermute | solution.py:25
where the time goes:
time: 390 us; the launch traced here: 389 us
  local copies, waits for them, and re-layouts  204 us (52%)
  other arithmetic  126 us (32%)
  starting transfers between devices  45.6 us (12%)
  waiting for transfers between devices  12.4 us (3%)
    gather x1, local copies, waits for them, and re-layouts, on_device(): seen = settled[3].reshape(ncell)[parcel_cell]  90.5 us
    scatter-add x1, other arithmetic, on_device(): release = jnp.zeros((ncell,), jnp.float32).at[parcel_dest].add(jnp.where(...  86.1 us
    scatter x1, local copies, waits for them, and re-layouts, on_device(): dest_buf = jnp.zeros((2 * slots + 1,), jnp.int32).at[index].set(parcel_de...  60.4 us
    scatter x1, local copies, waits for them, and re-layouts, on_device(): jnp.zeros((3, 2 * slots + 1), jnp.float32).at[:, index].set(records)  41.4 us
    scatter-add x1, other arithmetic, on_device(): release = release.at[arrived_cells].add(arrived_burn)  27.7 us
    ppermute x4, starting transfers between devices, shifted(): return lax.ppermute(block, axis, route)  17.5 us
    ppermute x4, starting transfers between devices, padded_2(): before = lax.ppermute(last, axis, up)  16 us
    ppermute x4, starting transfers between devices, padded_2(): after = lax.ppermute(initial, axis, down)  12.1 us
  transfers between devices with their start and end apart: 12, of which 3 were waited for; matrix products, arithmetic and copies ran while one was open for 39% of the time, Pallas kernels for 0%

commit v1 on v0

v1 whole, which is shorter than its diff:
```python
import jax
import jax.numpy as jnp
from jax import lax
from jax.experimental import pallas as pl
from jax.experimental.pallas import tpu as pltpu
from jax.sharding import PartitionSpec as P
F32=jnp.float32; BF=jnp.bfloat16

def iota_bf(n):
    return lax.broadcasted_iota(jnp.int32,(n,128),0).astype(F32).astype(BF)

def wide(row, n):
    t = jnp.broadcast_to(row,(16,128)).astype(BF)
    return jnp.concatenate([t]*(n//16),axis=0)

def split(x):
    hi = x.astype(BF).astype(F32)
    return hi, x-hi

def table(T, tab_ref):
    hi, lo = split(T)
    m = jnp.concatenate([hi[:, :256], hi[:, 256:], lo[:, :256], lo[:, 256:]], axis=0)
    tab_ref[...] = m.T.astype(BF)

def gather_block(b, rows, mode, cell_ref, tab_ref, seen_ref):
    cell = cell_ref[pl.ds(pl.multiple_of(b*rows,8), rows), :]
    key = (((cell >> 8) & 1) * 128 + (cell >> 9)).astype(F32)
    lo = (cell & 255).astype(F32)
    it = iota_bf(256)
    one = jnp.ones((256,128),BF); zero=jnp.zeros((256,128),BF)
    oh = jnp.concatenate([jnp.where(it == wide(key[i:i+1],256), one, zero) for i in range(rows)],axis=1)
    if mode == 0:
        res = jnp.dot(tab_ref[...], jnp.concatenate([oh,oh],axis=0), preferred_element_type=F32)
    else:
        res = jnp.dot(tab_ref[:, :256], oh, preferred_element_type=F32) + jnp.dot(tab_ref[:, 256:], oh, preferred_element_type=F32)
    itf = lax.broadcasted_iota(jnp.int32,(256,128),0).astype(F32)
    out = []
    for i in range(rows):
        r = res[:, i*128:(i+1)*128]
        out.append(jnp.sum(jnp.where(itf == lo[i:i+1], r, 0.0),axis=0,keepdims=True))
    seen_ref[pl.ds(pl.multiple_of(b*rows,8), rows), :] = jnp.concatenate(out,axis=0)

def burn_all(state_ref, seen, slot, out_ref, rec_ref):
    mass = state_ref[pl.ds(0,128,stride=2),:]
    temper = state_ref[pl.ds(1,128,stride=2),:]
    hot = temper + 0.3*(seen-temper)
    burned = 0.2*mass*(1.0+0.5*jnp.tanh(hot))
    left = mass-burned
    warm = hot+0.5*burned
    out_ref[pl.ds(0,128,stride=2),:] = left
    out_ref[pl.ds(1,128,stride=2),:] = warm
    rec_ref[0]=left; rec_ref[1]=warm; rec_ref[2]=burned

NT=(((1,),(1,)),((),()))

def compact_block(b, rows, slot_ref, dest_ref, rec_ref, acc_ref):
    ds = pl.ds(pl.multiple_of(b*rows,8), rows)
    slot = slot_ref[ds,:]; dest = dest_ref[ds,:]
    hi = (slot>>8).astype(F32); lo=(slot&255).astype(F32)
    vals=[]
    for f in range(3):
        vals += list(split(rec_ref[f, ds, :]))
    vals += [(dest>>8).astype(F32), (dest&255).astype(F32)]
    it = iota_bf(256); it16 = iota_bf(16)
    one = jnp.ones((256,128),BF); zero=jnp.zeros((256,128),BF)
    z16=jnp.zeros((16,128),BF)
    As=[];Bs=[]
    for i in range(rows):
        Bs.append(jnp.where(it == wide(lo[i:i+1],256), one, zero))
        m = it16 == wide(hi[i:i+1],16)
        As.append(jnp.concatenate([jnp.where(m, wide(v[i:i+1],16), z16) for v in vals],axis=0))
    A=jnp.concatenate(As,axis=1); B=jnp.concatenate(Bs,axis=1)
    acc_ref[...] += lax.dot_general(A,B,NT,preferred_element_type=F32)

def deposit_block(dest, burned, rows, acc_ref):
    hi=(((dest >> 8) & 1) * 128 + (dest >> 9)).astype(F32); lo=(dest&255).astype(F32)
    bh, bl = split(burned)
    it = iota_bf(256)
    one = jnp.ones((256,128),BF); zero=jnp.zeros((256,128),BF)
    As=[];Bs=[]
    for i in range(rows):
        Bs.append(jnp.where(it == wide(lo[i:i+1],256), one, zero))
        m = it == wide(hi[i:i+1],256)
        As.append(jnp.concatenate([jnp.where(m, wide(bh[i:i+1],256), zero),jnp.where(m, wide(bl[i:i+1],256), zero)],axis=0))
    A=jnp.concatenate(As,axis=1); B=jnp.concatenate(Bs,axis=1)
    acc_ref[...] += lax.dot_general(A,B,NT,preferred_element_type=F32)


def padded_2(x, sides, width):
    for axis, dim in sides:
        devices, length = (lax.axis_size(axis), x.shape[dim])
        up = [(i, (i + 1) % devices) for i in range(devices - 1)]
        down = [(j, i) for i, j in up]
        last = lax.slice_in_dim(x, length - width, length, axis=dim)
        initial = lax.slice_in_dim(x, 0, width, axis=dim)
        before = lax.ppermute(last, axis, up)
        after = lax.ppermute(initial, axis, down)
        x = jnp.concatenate([before, x, after], axis=dim)
    return x


def shifted(block, axis, distance):
    devices = range(lax.axis_size(axis))
    route = [(i - distance, i) for i in devices if i - distance in devices]
    return lax.ppermute(block, axis, route)


def advance(padded):
    zpad = jnp.pad(padded, ((0, 0), (0, 0), (0, 0), (1, 1)))
    center = zpad[:, 1:-1, 1:-1, 1:-1]
    xplus = zpad[:, 2:, 1:-1, 1:-1]
    xminus = zpad[:, :-2, 1:-1, 1:-1]
    yplus = zpad[:, 1:-1, 2:, 1:-1]
    yminus = zpad[:, 1:-1, :-2, 1:-1]
    zplus = zpad[:, 1:-1, 1:-1, 2:]
    zminus = zpad[:, 1:-1, 1:-1, :-2]
    carry_x = center[0:1]
    carry_y = center[1:2]
    carry_z = center[2:3]
    advect = 0.5 * (
        carry_x * (xplus - xminus) + carry_y * (yplus - yminus) + carry_z * (zplus - zminus)
    )
    laplace = xplus + xminus + yplus + yminus + zplus + zminus - 6.0 * center
    fresh = center - 0.1 * advect + 0.12 * laplace
    return fresh.at[2].add(0.1 * center[3])


SUBSTEPS = 2
ROWS = 16
VM = pl.BlockSpec(memory_space=pltpu.VMEM)


def parcels_kernel(temp_ref, cell_ref, dest_ref, slot_ref, state_ref, out_ref, box_ref, rel_ref, tab, seen, rec, acc):
    table(temp_ref[...], tab)
    steps = 128 // ROWS

    def gather(b, c):
        gather_block(b, ROWS, 1, cell_ref, tab, seen)
        return c
    lax.fori_loop(0, steps, gather, 0)
    burn_all(state_ref, seen[...], slot_ref[...], out_ref, rec)
    acc[...] = jnp.zeros_like(acc)

    def compact(b, c):
        compact_block(b, ROWS, slot_ref, dest_ref, rec, acc)
        return c
    lax.fori_loop(0, steps, compact, 0)
    for f in range(4):
        first, second = acc[32 * f:32 * f + 16, :], acc[32 * f + 16:32 * f + 32, :]
        both = first * 256.0 + second if f == 3 else first + second
        box_ref[0, f] = both[:8]
        box_ref[1, f] = both[8:]
    rel_ref[...] = jnp.zeros_like(rel_ref)

    def deposit(b, c):
        ds = pl.ds(pl.multiple_of(b * ROWS, 8), ROWS)
        burned = jnp.where(slot_ref[ds, :] < 0, rec[2, ds, :], 0.0)
        deposit_block(dest_ref[ds, :], burned, ROWS, rel_ref)
        return c
    lax.fori_loop(0, steps, deposit, 0)


def finish_kernel(low_ref, high_ref, rel_ref, gas_ref, out_ref, acc):
    acc[...] = rel_ref[...]
    for ref in (low_ref, high_ref):
        dest = ref[3].astype(jnp.int32)
        burned = jnp.concatenate([ref[2][:, :128], ref[2][:, 128:]], axis=0)
        dest = jnp.concatenate([dest[:, :128], dest[:, 128:]], axis=0)
        deposit_block(dest, burned, 16, acc)
    both = acc[:256, :] + acc[256:, :]
    release = jnp.concatenate([both[:128], both[128:]], axis=1).reshape(4, 32, 512)
    out_ref[0:3] = gas_ref[0:3]
    out_ref[3] = gas_ref[3] + 1.5 * release
    out_ref[4] = gas_ref[4] + release


def on_device(gas, parcel_state, parcel_cell, parcel_dest, send_slot, face_counts):
    rows, cols, depth = gas.shape[1:]
    settled = gas
    for step in range(SUBSTEPS):
        padded = padded_2(settled, (("prop", 1), ("cross", 2)), 1)
        settled = advance(padded)
    square = lambda a: a.reshape(128, 128)
    state = parcel_state.reshape(2, 128, 128).transpose(1, 0, 2).reshape(256, 128)
    params = pltpu.CompilerParams(vmem_limit_bytes=40 << 20)
    out, box, rel = pl.pallas_call(
        parcels_kernel,
        out_shape=(jax.ShapeDtypeStruct((256, 128), F32), jax.ShapeDtypeStruct((2, 4, 8, 256), F32), jax.ShapeDtypeStruct((512, 256), F32)),
        in_specs=[VM] * 5, out_specs=(VM, VM, VM),
        scratch_shapes=[pltpu.VMEM((256, 512), BF), pltpu.VMEM((128, 128), F32), pltpu.VMEM((3, 128, 128), F32), pltpu.VMEM((128, 256), F32)],
        compiler_params=params, name="parcels",
    )(settled[3].reshape(128, 512), square(parcel_cell), square(parcel_dest), square(send_slot), state)
    parcels_out = out.reshape(128, 2, 128).transpose(1, 0, 2).reshape(2, 16384)
    slots = 2048
    counts = face_counts.reshape(2)
    live = jnp.arange(slots, dtype=jnp.int32).reshape(8, 256)[None] < counts[:, None, None]
    box = jnp.where(live[:, None], box, 0.0)
    low = shifted(box[1], "prop", 1)
    high = shifted(box[0], "prop", -1)
    gas_out = pl.pallas_call(
        finish_kernel, out_shape=jax.ShapeDtypeStruct(gas.shape, F32),
        in_specs=[VM] * 4, out_specs=VM, scratch_shapes=[pltpu.VMEM((512, 256), F32)],
        compiler_params=params, name="finish",
    )(low, high, rel, settled)
    arrivals = jnp.stack([low[:3].reshape(3, slots), high[:3].reshape(3, slots)], axis=0)
    return (gas_out, parcels_out, arrivals)


def solution(mesh):
    in_specs = (
        P(None, "prop", "cross", None),
        P(None, ("prop", "cross")),
        P(("prop", "cross")),
        P(("prop", "cross")),
        P(("prop", "cross")),
        P("prop", "cross", None),
    )
    out_specs = (
        P(None, "prop", "cross", None),
        P(None, ("prop", "cross")),
        P(None, None, ("prop", "cross")),
    )
    return jax.shard_map(
        on_device, mesh=mesh, in_specs=in_specs, out_specs=out_specs, check_vma=False
    )
```

time: 390 us -> 92.8 us (0.24)
  local copies, waits for them, and re-layouts: 204 us -> 3.18 us
  other arithmetic: 126 us -> 6.47 us
  Pallas kernels: 0 us -> 18.3 us
  waiting for transfers between devices: 12.4 us -> 27 us
  starting transfers between devices: 45.6 us -> 36.5 us
    scatter-add x2 -> x0, other arithmetic: 114 us -> none  [the longest x1 86.1 us: on_device(): release = jnp.zeros((ncell,), jnp.float32).at[parcel_dest].add(jnp.where(...]
    scatter x2 -> x0, local copies, waits for them, and re-layouts: 102 us -> none  [the longest x1 60.4 us: on_device(): dest_buf = jnp.zeros((2 * slots + 1,), jnp.int32).at[index].set(parcel_de...]
    gather x1 -> x0, local copies, waits for them, and re-layouts: 90.5 us -> none  [on_device(): seen = settled[3].reshape(ncell)[parcel_cell]]
    pallas_call x0 -> x2, Pallas kernels: none -> 18.3 us  [the longest x1 15.9 us: on_device(): pl.pallas_call(parcels_kernel, out_shape=(jax.ShapeDtypeStruct((256, 128)...]
    ppermute x4 -> x2, starting transfers between devices: 17.5 us -> 10.4 us  [shifted(): return lax.ppermute(block, axis, route)]
    ppermute x4 -> x2, waiting for transfers between devices: 0.01 us -> 5.67 us  [shifted(): return lax.ppermute(block, axis, route)]
    ppermute x4, waiting for transfers between devices: 3.67 us -> 9.19 us  [padded_2(): after = lax.ppermute(initial, axis, down)]
    another operation x1 -> x2, local copies, waits for them, and re-layouts: 5.03 us -> 0.04 us  [on_device(): jnp.stack([low[:3].reshape(3, slots), high[:3].reshape(3, slots)], axis=0)]
  transfers between devices with their start and end apart: 12 -> 10, of which waited for: 3 -> 7; matrix products, arithmetic and copies ran while one was open for 39% -> 0% of each run, Pallas kernels for 0% -> 0%
where the time goes in v1:
time: 92.8 us; the launch traced here: 92.4 us
  starting transfers between devices  36.5 us (39%)
  waiting for transfers between devices  27 us (29%)
  Pallas kernels  18.3 us (20%)
  other arithmetic  6.47 us (7%)
  local copies, waits for them, and re-layouts  3.18 us (3%)
  between operations  0.95 us (1%)
    ppermute x4, starting transfers between devices, padded_2(): before = lax.ppermute(last, axis, up)  16.3 us
    pallas_call x1, Pallas kernels, on_device(): pl.pallas_call(parcels_kernel, out_shape=(jax.ShapeDtypeStruct((256, 128)...  15.9 us
    ppermute x4, waiting for transfers between devices, padded_2(): before = lax.ppermute(last, axis, up)  12.2 us
    ppermute x2, starting transfers between devices, shifted(): return lax.ppermute(block, axis, route)  10.4 us
    ppermute x4, starting transfers between devices, padded_2(): after = lax.ppermute(initial, axis, down)  9.77 us
    ppermute x4, waiting for transfers between devices, padded_2(): after = lax.ppermute(initial, axis, down)  9.19 us
    ppermute x2, waiting for transfers between devices, shifted(): return lax.ppermute(block, axis, route)  5.67 us
    add x2, other arithmetic, advance(): fresh = center - 0.1 * advect + 0.12 * laplace  3.27 us
  transfers between devices with their start and end apart: 10, of which 7 were waited for; matrix products, arithmetic and copies ran while one was open for 0% of the time, Pallas kernels for 0%

profile of v1, /device:TPU:7, one launch (start us, length us, event | category | flops | bytes accessed | tf_op | source)
XLA Modules:
  0.0 92.4 jit_solution(12341225876190413910)
XLA Ops:
  0.6 0.0 copy-start.4
  0.6 1.2 %fusion.7 = (f32[5,1,32,512]{3,2,1,0:T(8,128)S(1)}, f32[5,1,32,512]{3,2,1,0:T(8,128)S(1)}) fusion(f32[5,4,32,512]{3,2,1,0:T(8,128)} %param.10), kind=kLoop, calls=%fused_computation.48 | loop fusion | bytes 1310720 | tf_op jit(solution)/shard_map/slice | solution.py:95
  1.9 4.9 %collective-permute-start.1 = (f32[5,1,32,512]{3,2,1,0:T(8,128)S(1)}, f32[5,1,32,512]{3,2,1,0:T(8,128)S(1)}, u32[]{:S(2)}, u32[]{:S(2)}) collective-permute-start(f32[5,1,32,512]{3,2,1,0:T(8,128)S(1)} %get-tuple-element.50), channel_id=1, source_target_pairs={{0,8},{8,16},{16,24},{24,32},{32,40},{40,48},{48,56},{56,64},{64,7... | collective-permute-start | bytes 983048 | tf_op jit(solution)/shard_map/ppermute | solution.py:96
  6.8 1.9 %collective-permute-start = (f32[5,1,32,512]{3,2,1,0:T(8,128)S(1)}, f32[5,1,32,512]{3,2,1,0:T(8,128)S(1)}, u32[]{:S(2)}, u32[]{:S(2)}) collective-permute-start(f32[5,1,32,512]{3,2,1,0:T(8,128)S(1)} %get-tuple-element.49), channel_id=1, source_target_pairs={{8,0},{16,8},{24,16},{32,24},{40,32},{48,40},{56,48},{64,56},{72,6... | collective-permute-start | bytes 983048 | tf_op jit(solution)/shard_map/ppermute | solution.py:97
  8.8 2.5 %collective-permute-done.1 = f32[5,1,32,512]{3,2,1,0:T(8,128)S(1)} collective-permute-done((f32[5,1,32,512]{3,2,1,0:T(8,128)S(1)}, f32[5,1,32,512]{3,2,1,0:T(8,128)S(1)}, u32[]{:S(2)}, u32[]{:S(2)}) %collective-permute-start.1) | collective-permute-done | bytes 327712 | tf_op jit(solution)/shard_map/ppermute | solution.py:96
  11.3 0.0 copy-done.4
  11.3 0.1 constant_dynamic-update-slice_fusion.1
  11.4 6.2 %collective-permute-done = f32[5,1,32,512]{3,2,1,0:T(8,128)S(1)} collective-permute-done((f32[5,1,32,512]{3,2,1,0:T(8,128)S(1)}, f32[5,1,32,512]{3,2,1,0:T(8,128)S(1)}, u32[]{:S(2)}, u32[]{:S(2)}) %collective-permute-start) | collective-permute-done | bytes 327712 | tf_op jit(solution)/shard_map/ppermute | solution.py:97
  17.6 0.1 fusion.5
  17.8 4.0 %collective-permute-start.2 = (f32[5,6,1,512]{3,2,1,0:T(1,128)S(1)}, f32[5,6,1,512]{3,2,1,0:T(1,128)S(1)}, u32[]{:S(2)}, u32[]{:S(2)}) collective-permute-start(f32[5,6,1,512]{3,2,1,0:T(1,128)S(1)} %get-tuple-element.41), channel_id=1, source_target_pairs={{1,0},{2,1},{3,2},{4,3},{5,4},{6,5},{7,6},{9,8},{10,9},{11,10},{12... | collective-permute-start | bytes 184328 | tf_op jit(solution)/shard_map/ppermute | solution.py:97
  21.8 1.9 %collective-permute-start.3 = (f32[5,6,1,512]{3,2,1,0:T(1,128)S(1)}, f32[5,6,1,512]{3,2,1,0:T(1,128)S(1)}, u32[]{:S(2)}, u32[]{:S(2)}) collective-permute-start(f32[5,6,1,512]{3,2,1,0:T(1,128)S(1)} %get-tuple-element.40), channel_id=1, source_target_pairs={{0,1},{1,2},{2,3},{3,4},{4,5},{5,6},{6,7},{8,9},{9,10},{10,11},{11... | collective-permute-start | bytes 184328 | tf_op jit(solution)/shard_map/ppermute | solution.py:96
  23.7 0.1 slice_bitcast_fusion.4
  23.8 0.0 collective-permute-done.2
  23.8 5.1 %collective-permute-done.3 = f32[5,6,1,512]{3,2,1,0:T(1,128)S(1)} collective-permute-done((f32[5,6,1,512]{3,2,1,0:T(1,128)S(1)}, f32[5,6,1,512]{3,2,1,0:T(1,128)S(1)}, u32[]{:S(2)}, u32[]{:S(2)}) %collective-permute-start.3) | collective-permute-done | bytes 61472 | tf_op jit(solution)/shard_map/ppermute | solution.py:96
  28.9 1.4 %select_maximum_fusion.4 = f32[5,6,34,514]{3,2,1,0:T(8,128)S(1)} fusion(f32[5,6,1,512]{3,2,1,0:T(1,128)S(1)} %collective-permute-done.2, f32[5,6,32,512]{3,2,1,0:T(8,128)S(1)} %constant_dynamic-update-slice_fusion, f32[5,6,1,512]{3,2,1,0:T(1,128)S(1)} %collective-permute-done.3), kind=kLoop, calls=%fused_computation.6 | loop fusion | flops 4194240 | bytes 4186080 | tf_op jit(solution)/shard_map/concatenate | solution.py:98
  30.3 1.5 %multiply_add_fusion.1 = f32[5,4,32,512]{3,2,1,0:T(8,128)S(1)} fusion(f32[5,4,32,512]{3,2,1,0:T(8,128)S(1)} %copy-done.4, f32[5,6,34,514]{3,2,1,0:T(8,128)S(1)} %select_maximum_fusion.4, f32[5,6,1,512]{3,2,1,0:T(1,128)S(1)} %collective-permute-done.2, f32[5,6,32,512]{3,2,1,0:T(8,128)S(1)} %constant_dynamic-update-slice_fusion, ...), kind=kLoop, calls=%fused_computation.22 | loop fusion | flops 7536640 | bytes 8773632 | tf_op jit(solution)/shard_map/add | solution.py:124
  31.8 0.0 copy-start.5
  31.8 0.1 fusion.3
  32.0 1.9 %collective-permute-start.4 = (f32[5,1,32,512]{3,2,1,0:T(8,128)S(1)}, f32[5,1,32,512]{3,2,1,0:T(8,128)S(1)}, u32[]{:S(2)}, u32[]{:S(2)}) collective-permute-start(f32[5,1,32,512]{3,2,1,0:T(8,128)S(1)} %get-tuple-element.45), channel_id=1, source_target_pairs={{8,0},{16,8},{24,16},{32,24},{40,32},{48,40},{56,48},{64,56},{72,6... | collective-permute-start | bytes 983048 | tf_op jit(solution)/shard_map/ppermute | solution.py:97
  33.9 6.0 %collective-permute-start.5 = (f32[5,1,32,512]{3,2,1,0:T(8,128)S(1)}, f32[5,1,32,512]{3,2,1,0:T(8,128)S(1)}, u32[]{:S(2)}, u32[]{:S(2)}) collective-permute-start(f32[5,1,32,512]{3,2,1,0:T(8,128)S(1)} %get-tuple-element.44), channel_id=1, source_target_pairs={{0,8},{8,16},{16,24},{24,32},{32,40},{40,48},{48,56},{56,64},{64,7... | collective-permute-start | bytes 983048 | tf_op jit(solution)/shard_map/ppermute | solution.py:96
  40.0 0.0 copy-done.5
  40.0 0.1 broadcast_compare_fusion
  40.1 3.0 %collective-permute-done.4 = f32[5,1,32,512]{3,2,1,0:T(8,128)S(1)} collective-permute-done((f32[5,1,32,512]{3,2,1,0:T(8,128)S(1)}, f32[5,1,32,512]{3,2,1,0:T(8,128)S(1)}, u32[]{:S(2)}, u32[]{:S(2)}) %collective-permute-start.4) | collective-permute-done | bytes 327712 | tf_op jit(solution)/shard_map/ppermute | solution.py:97
  43.0 0.9 collective-permute-done.5
  44.0 0.1 pad_maximum_fusion.13
  44.1 1.9 %collective-permute-start.6 = (f32[5,6,1,512]{3,2,1,0:T(1,128)S(1)}, f32[5,6,1,512]{3,2,1,0:T(1,128)S(1)}, u32[]{:S(2)}, u32[]{:S(2)}) collective-permute-start(f32[5,6,1,512]{3,2,1,0:T(1,128)S(1)} %get-tuple-element.39), channel_id=1, source_target_pairs={{1,0},{2,1},{3,2},{4,3},{5,4},{6,5},{7,6},{9,8},{10,9},{11,10},{12... | collective-permute-start | bytes 184328 | tf_op jit(solution)/shard_map/ppermute | solution.py:97
  46.0 3.4 %collective-permute-start.7 = (f32[5,6,1,512]{3,2,1,0:T(1,128)S(1)}, f32[5,6,1,512]{3,2,1,0:T(1,128)S(1)}, u32[]{:S(2)}, u32[]{:S(2)}) collective-permute-start(f32[5,6,1,512]{3,2,1,0:T(1,128)S(1)} %get-tuple-element.38), channel_id=1, source_target_pairs={{0,1},{1,2},{2,3},{3,4},{4,5},{5,6},{6,7},{8,9},{9,10},{10,11},{11... | collective-permute-start | bytes 184328 | tf_op jit(solution)/shard_map/ppermute | solution.py:96
  49.4 0.0 collective-permute-done.6
  49.4 3.7 %collective-permute-done.7 = f32[5,6,1,512]{3,2,1,0:T(1,128)S(1)} collective-permute-done((f32[5,6,1,512]{3,2,1,0:T(1,128)S(1)}, f32[5,6,1,512]{3,2,1,0:T(1,128)S(1)}, u32[]{:S(2)}, u32[]{:S(2)}) %collective-permute-start.7) | collective-permute-done | bytes 61472 | tf_op jit(solution)/shard_map/ppermute | solution.py:96
  53.1 1.4 %select_maximum_fusion = f32[5,6,34,514]{3,2,1,0:T(8,128)S(1)} fusion(f32[5,6,1,512]{3,2,1,0:T(1,128)S(1)} %collective-permute-done.6, f32[5,6,1,512]{3,2,1,0:T(1,128)S(1)} %collective-permute-done.7, f32[5,1,32,512]{3,2,1,0:T(8,128)S(1)} %collective-permute-done.4, f32[5,4,32,512]{3,2,1,0:T(8,128)S(1)} %get-tuple-element.37, ...), kind=kLoop, calls=%fused_computation.2 | loop fusion | flops 6291360 | bytes 4186080 | tf_op jit(solution)/shard_map/concatenate | solution.py:98
  54.5 1.7 %multiply_add_fusion = f32[5,4,32,512]{3,2,1,0:T(8,128)S(1)} fusion(f32[5,4,32,512]{3,2,1,0:T(8,128)S(1)} %get-tuple-element.37, f32[5,6,34,514]{3,2,1,0:T(8,128)S(1)} %select_maximum_fusion, f32[5,6,1,512]{3,2,1,0:T(1,128)S(1)} %collective-permute-done.6, f32[5,1,32,512]{3,2,1,0:T(8,128)S(1)} %collective-permute-done.4, ...), kind=kLoop, calls=%fused_computation.21 | loop fusion | flops 8847360 | bytes 6807552 | tf_op jit(solution)/shard_map/add | solution.py:124
  56.2 0.0 copy-start
  56.2 0.0 copy-start.1
  56.2 0.0 copy-start.2
  56.3 0.0 copy-start.3
  56.3 0.1 fusion.2.gas_ref
  56.4 0.8 copy-done
  57.1 0.0 copy-done.1
  57.1 0.0 copy-done.2
  57.2 0.0 copy-done.3
  57.2 15.9 %parcels.1 = (f32[256,128]{1,0:T(8,128)}, f32[2,4,8,256]{3,2,1,0:T(8,128)S(1)}, f32[512,256]{1,0:T(8,128)S(1)}) custom-call(f32[128,512]{1,0:T(8,128)S(1)} %bitcast.31, s32[128,128]{1,0:T(8,128)S(1)} %bitcast.33, s32[128,128]{1,0:T(8,128)S(1)} %bitcast.34, s32[128,128]{1,0:T(8,128)S(1)} %bitcast.35, f32[256,128]{1,0:T(8,128)S(1)} %bitcast.32), custom_call_target="tpu_custom_call" | custom-call | tf_op jit(solution)/shard_map/parcels/pallas_call | solution.py:186
  73.2 8.5 %collective-permute-start.8 = (f32[4,8,256]{2,1,0:T(8,128)S(1)}, f32[4,8,256]{2,1,0:T(8,128)S(1)}, u32[]{:S(2)}, u32[]{:S(2)}) collective-permute-start(f32[4,8,256]{2,1,0:T(8,128)S(1)} %get-tuple-element.52), channel_id=1, source_target_pairs={{0,8},{8,16},{16,24},{24,32},{32,40},{40,48},{48,56},{56,64},{64,7... | collective-permute-start | bytes 98312 | tf_op jit(solution)/shard_map/ppermute | solution.py:105
  81.7 1.9 %collective-permute-start.9 = (f32[4,8,256]{2,1,0:T(8,128)S(1)}, f32[4,8,256]{2,1,0:T(8,128)S(1)}, u32[]{:S(2)}, u32[]{:S(2)}) collective-permute-start(f32[4,8,256]{2,1,0:T(8,128)S(1)} %get-tuple-element.51), channel_id=1, source_target_pairs={{8,0},{16,8},{24,16},{32,24},{40,32},{48,40},{56,48},{64,56},{72,6... | collective-permute-start | bytes 98312 | tf_op jit(solution)/shard_map/ppermute | solution.py:105
  83.6 0.0 collective-permute-done.8.low_ref
  83.6 5.7 %collective-permute-done.9.high_ref = f32[4,8,256]{2,1,0:T(8,128)S(1)} collective-permute-done((f32[4,8,256]{2,1,0:T(8,128)S(1)}, f32[4,8,256]{2,1,0:T(8,128)S(1)}, u32[]{:S(2)}, u32[]{:S(2)}) %collective-permute-start.9) | collective-permute-done | bytes 32800 | tf_op jit(solution)/shard_map/ppermute | solution.py:105
  89.4 0.7 copy.15
  90.0 2.4 %finish.1 = f32[5,4,32,512]{3,2,1,0:T(8,128)} custom-call(f32[4,8,256]{2,1,0:T(8,128)S(1)} %collective-permute-done.8.low_ref, f32[4,8,256]{2,1,0:T(8,128)S(1)} %collective-permute-done.9.high_ref, f32[512,256]{1,0:T(8,128)S(1)} %get-tuple-element.31.rel_ref, f32[5,4,32,512]{3,2,1,0:T(8,128)S(1)} %fusion.2.gas_ref), custom_call_target="tpu_custom_call" | custom-call | tf_op jit(solution)/shard_map/finish/pallas_call | solution.py:200
  (13 shorter events, 0.2 us)
Async XLA Ops:
  0.6 10.7 %copy-start.4 = (f32[5,4,32,512]{3,2,1,0:T(8,128)S(1)}, f32[5,4,32,512]{3,2,1,0:T(8,128)}, u32[]{:S(2)}) copy-start(f32[5,4,32,512]{3,2,1,0:T(8,128)} %param.10) | copy-start | bytes 3932164
  1.9 9.4 %collective-permute-start.1 = (f32[5,1,32,512]{3,2,1,0:T(8,128)S(1)}, f32[5,1,32,512]{3,2,1,0:T(8,128)S(1)}, u32[]{:S(2)}, u32[]{:S(2)}) collective-permute-start(f32[5,1,32,512]{3,2,1,0:T(8,128)S(1)} %get-tuple-element.50), channel_id=1, source_target_pairs={{0,8},{8,16},{16,24},{24,32},{32,40},{40,48},{48,56},{56,64},{64,7... | collective-permute-start | bytes 983048 | tf_op jit(solution)/shard_map/ppermute | solution.py:96
  6.8 10.8 %collective-permute-start = (f32[5,1,32,512]{3,2,1,0:T(8,128)S(1)}, f32[5,1,32,512]{3,2,1,0:T(8,128)S(1)}, u32[]{:S(2)}, u32[]{:S(2)}) collective-permute-start(f32[5,1,32,512]{3,2,1,0:T(8,128)S(1)} %get-tuple-element.49), channel_id=1, source_target_pairs={{8,0},{16,8},{24,16},{32,24},{40,32},{48,40},{56,48},{64,56},{72,6... | collective-permute-start | bytes 983048 | tf_op jit(solution)/shard_map/ppermute | solution.py:97
  17.8 6.0 %collective-permute-start.2 = (f32[5,6,1,512]{3,2,1,0:T(1,128)S(1)}, f32[5,6,1,512]{3,2,1,0:T(1,128)S(1)}, u32[]{:S(2)}, u32[]{:S(2)}) collective-permute-start(f32[5,6,1,512]{3,2,1,0:T(1,128)S(1)} %get-tuple-element.41), channel_id=1, source_target_pairs={{1,0},{2,1},{3,2},{4,3},{5,4},{6,5},{7,6},{9,8},{10,9},{11,10},{12... | collective-permute-start | bytes 184328 | tf_op jit(solution)/shard_map/ppermute | solution.py:97
  21.8 7.1 %collective-permute-start.3 = (f32[5,6,1,512]{3,2,1,0:T(1,128)S(1)}, f32[5,6,1,512]{3,2,1,0:T(1,128)S(1)}, u32[]{:S(2)}, u32[]{:S(2)}) collective-permute-start(f32[5,6,1,512]{3,2,1,0:T(1,128)S(1)} %get-tuple-element.40), channel_id=1, source_target_pairs={{0,1},{1,2},{2,3},{3,4},{4,5},{5,6},{6,7},{8,9},{9,10},{10,11},{11... | collective-permute-start | bytes 184328 | tf_op jit(solution)/shard_map/ppermute | solution.py:96
  31.8 8.2 %copy-start.5 = (s32[1,1,2]{2,1,0:T(1,128)S(1)}, s32[1,1,2]{2,1,0:T(1,128)}, u32[]{:S(2)}) copy-start(s32[1,1,2]{2,1,0:T(1,128)} %param.15) | copy-start | bytes 28
  32.0 11.1 %collective-permute-start.4 = (f32[5,1,32,512]{3,2,1,0:T(8,128)S(1)}, f32[5,1,32,512]{3,2,1,0:T(8,128)S(1)}, u32[]{:S(2)}, u32[]{:S(2)}) collective-permute-start(f32[5,1,32,512]{3,2,1,0:T(8,128)S(1)} %get-tuple-element.45), channel_id=1, source_target_pairs={{8,0},{16,8},{24,16},{32,24},{40,32},{48,40},{56,48},{64,56},{72,6... | collective-permute-start | bytes 983048 | tf_op jit(solution)/shard_map/ppermute | solution.py:97
  33.9 10.1 %collective-permute-start.5 = (f32[5,1,32,512]{3,2,1,0:T(8,128)S(1)}, f32[5,1,32,512]{3,2,1,0:T(8,128)S(1)}, u32[]{:S(2)}, u32[]{:S(2)}) collective-permute-start(f32[5,1,32,512]{3,2,1,0:T(8,128)S(1)} %get-tuple-element.44), channel_id=1, source_target_pairs={{0,8},{8,16},{16,24},{24,32},{32,40},{40,48},{48,56},{56,64},{64,7... | collective-permute-start | bytes 983048 | tf_op jit(solution)/shard_map/ppermute | solution.py:96
  44.1 5.3 %collective-permute-start.6 = (f32[5,6,1,512]{3,2,1,0:T(1,128)S(1)}, f32[5,6,1,512]{3,2,1,0:T(1,128)S(1)}, u32[]{:S(2)}, u32[]{:S(2)}) collective-permute-start(f32[5,6,1,512]{3,2,1,0:T(1,128)S(1)} %get-tuple-element.39), channel_id=1, source_target_pairs={{1,0},{2,1},{3,2},{4,3},{5,4},{6,5},{7,6},{9,8},{10,9},{11,10},{12... | collective-permute-start | bytes 184328 | tf_op jit(solution)/shard_map/ppermute | solution.py:97
  46.0 7.1 %collective-permute-start.7 = (f32[5,6,1,512]{3,2,1,0:T(1,128)S(1)}, f32[5,6,1,512]{3,2,1,0:T(1,128)S(1)}, u32[]{:S(2)}, u32[]{:S(2)}) collective-permute-start(f32[5,6,1,512]{3,2,1,0:T(1,128)S(1)} %get-tuple-element.38), channel_id=1, source_target_pairs={{0,1},{1,2},{2,3},{3,4},{4,5},{5,6},{6,7},{8,9},{9,10},{10,11},{11... | collective-permute-start | bytes 184328 | tf_op jit(solution)/shard_map/ppermute | solution.py:96
  56.2 0.9 copy-start
  56.2 0.9 copy-start.1
  56.2 0.9 copy-start.2
  56.3 0.9 %copy-start.3 = (s32[16384]{0:T(1024)S(1)}, s32[16384]{0:T(1024)}, u32[]{:S(2)}) copy-start(s32[16384]{0:T(1024)} %param.14) | copy-start | bytes 196612
  73.2 10.4 %collective-permute-start.8 = (f32[4,8,256]{2,1,0:T(8,128)S(1)}, f32[4,8,256]{2,1,0:T(8,128)S(1)}, u32[]{:S(2)}, u32[]{:S(2)}) collective-permute-start(f32[4,8,256]{2,1,0:T(8,128)S(1)} %get-tuple-element.52), channel_id=1, source_target_pairs={{0,8},{8,16},{16,24},{24,32},{32,40},{40,48},{48,56},{56,64},{64,7... | collective-permute-start | bytes 98312 | tf_op jit(solution)/shard_map/ppermute | solution.py:105
  81.7 7.6 %collective-permute-start.9 = (f32[4,8,256]{2,1,0:T(8,128)S(1)}, f32[4,8,256]{2,1,0:T(8,128)S(1)}, u32[]{:S(2)}, u32[]{:S(2)}) collective-permute-start(f32[4,8,256]{2,1,0:T(8,128)S(1)} %get-tuple-element.51), channel_id=1, source_target_pairs={{8,0},{16,8},{24,16},{32,24},{40,32},{48,40},{56,48},{64,56},{72,6... | collective-permute-start | bytes 98312 | tf_op jit(solution)/shard_map/ppermute | solution.py:105

commit v2 on v0

v2 whole, which is shorter than its diff:
```python
import functools
import jax
import jax.numpy as jnp
from jax import lax
from jax.experimental import pallas as pl
from jax.experimental.pallas import tpu as pltpu
from jax.sharding import PartitionSpec as P

F32 = jnp.float32
BF = jnp.bfloat16
ROWS = 16
NT = (((1,), (1,)), ((), ()))
GROUPS = ((3, 4), (0, 3), (4, 5))


def iota_bf(n):
    return lax.broadcasted_iota(jnp.int32, (n, 128), 0).astype(F32).astype(BF)


def wide(row, n):
    t = jnp.broadcast_to(row, (16, 128)).astype(BF)
    return jnp.concatenate([t] * (n // 16), axis=0)


def split(x):
    hi = x.astype(BF).astype(F32)
    return hi, x - hi


def key_of(cell):
    return (((cell >> 8) & 1) * 128 + (cell >> 9)).astype(F32)


def low_of(cell):
    return (cell & 255).astype(F32)


def table(T, tab_ref):
    hi, lo = split(T)
    m = jnp.concatenate([hi[:, :256], hi[:, 256:], lo[:, :256], lo[:, 256:]], axis=0)
    tab_ref[...] = m.T.astype(BF)


def gather_block(b, rows, cell_ref, tab_ref, seen_ref):
    cell = cell_ref[pl.ds(pl.multiple_of(b * rows, 8), rows), :]
    key = key_of(cell)
    lo = low_of(cell)
    it = iota_bf(256)
    one = jnp.ones((256, 128), BF)
    zero = jnp.zeros((256, 128), BF)
    oh = jnp.concatenate([jnp.where(it == wide(key[i:i + 1], 256), one, zero) for i in range(rows)], axis=1)
    res = jnp.dot(tab_ref[:, :256], oh, preferred_element_type=F32) + jnp.dot(tab_ref[:, 256:], oh, preferred_element_type=F32)
    itf = lax.broadcasted_iota(jnp.int32, (256, 128), 0).astype(F32)
    out = []
    for i in range(rows):
        r = res[:, i * 128:(i + 1) * 128]
        out.append(jnp.sum(jnp.where(itf == lo[i:i + 1], r, 0.0), axis=0, keepdims=True))
    seen_ref[pl.ds(pl.multiple_of(b * rows, 8), rows), :] = jnp.concatenate(out, axis=0)


def burn_all(state_ref, seen, out_ref, rec_ref):
    mass = state_ref[pl.ds(0, 128, stride=2), :]
    temper = state_ref[pl.ds(1, 128, stride=2), :]
    hot = temper + 0.3 * (seen - temper)
    burned = 0.2 * mass * (1.0 + 0.5 * jnp.tanh(hot))
    left = mass - burned
    warm = hot + 0.5 * burned
    out_ref[pl.ds(0, 128, stride=2), :] = left
    out_ref[pl.ds(1, 128, stride=2), :] = warm
    rec_ref[0] = left
    rec_ref[1] = warm
    rec_ref[2] = burned


def compact_block(b, rows, slot_ref, dest_ref, rec_ref, acc_ref):
    ds = pl.ds(pl.multiple_of(b * rows, 8), rows)
    slot = slot_ref[ds, :]
    dest = dest_ref[ds, :]
    hi = (slot >> 8).astype(F32)
    lo = (slot & 255).astype(F32)
    vals = []
    for f in range(3):
        vals += list(split(rec_ref[f, ds, :]))
    vals += [(dest >> 8).astype(F32), (dest & 255).astype(F32)]
    it = iota_bf(256)
    it16 = iota_bf(16)
    one = jnp.ones((256, 128), BF)
    zero = jnp.zeros((256, 128), BF)
    z16 = jnp.zeros((16, 128), BF)
    As, Bs = [], []
    for i in range(rows):
        Bs.append(jnp.where(it == wide(lo[i:i + 1], 256), one, zero))
        m = it16 == wide(hi[i:i + 1], 16)
        As.append(jnp.concatenate([jnp.where(m, wide(v[i:i + 1], 16), z16) for v in vals], axis=0))
    A = jnp.concatenate(As, axis=1)
    B = jnp.concatenate(Bs, axis=1)
    acc_ref[...] += lax.dot_general(A, B, NT, preferred_element_type=F32)


def deposit_block(dest, burned, rows, acc_ref):
    hi = key_of(dest)
    lo = low_of(dest)
    bh, bl = split(burned)
    it = iota_bf(256)
    one = jnp.ones((256, 128), BF)
    zero = jnp.zeros((256, 128), BF)
    As, Bs = [], []
    for i in range(rows):
        Bs.append(jnp.where(it == wide(lo[i:i + 1], 256), one, zero))
        m = it == wide(hi[i:i + 1], 256)
        As.append(jnp.concatenate([jnp.where(m, wide(bh[i:i + 1], 256), zero), jnp.where(m, wide(bl[i:i + 1], 256), zero)], axis=0))
    A = jnp.concatenate(As, axis=1)
    B = jnp.concatenate(Bs, axis=1)
    acc_ref[...] += lax.dot_general(A, B, NT, preferred_element_type=F32)


def plane(g, hy, f, i):
    c = g[f, i]
    rows, depth = c.shape
    row = lax.broadcasted_iota(jnp.int32, (rows, depth), 0)
    lane = lax.broadcasted_iota(jnp.int32, (rows, depth), 1)
    xm, xp = g[f, i - 1], g[f, i + 1]
    ym = jnp.where(row == 0, hy[f, 0, pl.ds(i - 1, 1), :], pltpu.roll(c, 1, 0))
    yp = jnp.where(row == rows - 1, hy[f, 1, pl.ds(i - 1, 1), :], pltpu.roll(c, rows - 1, 0))
    zm = jnp.where(lane == 0, 0.0, pltpu.roll(c, 1, 1))
    zp = jnp.where(lane == depth - 1, 0.0, pltpu.roll(c, depth - 1, 1))
    advect = g[0, i] * (xp - xm) + g[1, i] * (yp - ym) + g[2, i] * (zp - zm)
    laplace = (xp + xm) + (yp + ym) + (zp + zm) - 6.0 * c
    return c - 0.05 * advect + 0.12 * laplace


def step_kernel(gas_hbm, cell_hbm, dest_hbm, slot_hbm, state_hbm, counts_ref,
                gas_out, state_out, arr_out,
                g0, g1, t2, hy0, hy1, sy0, sy1, cell, dest, slot, state,
                tab, seen, rec, acc, rel, box, got,
                in_sem, xs, xr, ys, yr, fs, fr):
    p, c = lax.axis_index("prop"), lax.axis_index("cross")
    np_, nc = lax.axis_size("prop"), lax.axis_size("cross")
    below = {"prop": lax.rem(p + np_ - 1, np_)}
    above = {"prop": lax.rem(p + 1, np_)}
    left = {"cross": lax.rem(c + nc - 1, nc)}
    right = {"cross": lax.rem(c + 1, nc)}
    gs, hys, sys_ = (g0, g1), (hy0, hy1), (sy0, sy1)

    def remote(a, b, s, r, to):
        return pltpu.make_async_remote_copy(src_ref=a, dst_ref=b, send_sem=s, recv_sem=r, device_id=to, device_id_type=pl.DeviceIdType.MESH)

    def halo(r, k):
        lo, hi = GROUPS[k]
        fields = pl.ds(lo, hi - lo)
        if r == 0:
            first, last = gas_hbm.at[fields, 0], gas_hbm.at[fields, 3]
        else:
            first, last = g1.at[fields, 1], g1.at[fields, 4]
        sy, hy, g = sys_[r], hys[r], gs[r]
        return [
            remote(first, g.at[fields, 5], xs.at[r, k, 0], xr.at[r, k, 0], below),
            remote(last, g.at[fields, 0], xs.at[r, k, 1], xr.at[r, k, 1], above),
            remote(sy.at[fields, 0], hy.at[fields, 1], ys.at[r, k, 0], yr.at[r, k, 0], left),
            remote(sy.at[fields, 1], hy.at[fields, 0], ys.at[r, k, 1], yr.at[r, k, 1], right),
        ]

    def stage(r, f):
        for i in range(4):
            sys_[r][f, 0, i:i + 1, :] = gs[r][f, 1 + i, 0:1, :]
            sys_[r][f, 1, i:i + 1, :] = gs[r][f, 1 + i, 31:32, :]

    def send(r, k):
        for copy in halo(r, k):
            copy.start()

    def receive(r, k):
        for copy in halo(r, k):
            copy.wait_recv()
        lo, hi = GROUPS[k]

        @pl.when(p == 0)
        def _():
            for f in range(lo, hi):
                gs[r][f, 0] = jnp.zeros((32, 512), F32)

        @pl.when(p == np_ - 1)
        def _():
            for f in range(lo, hi):
                gs[r][f, 5] = jnp.zeros((32, 512), F32)

        @pl.when(c == 0)
        def _():
            for f in range(lo, hi):
                hys[r][f, 0] = jnp.zeros((4, 512), F32)

        @pl.when(c == nc - 1)
        def _():
            for f in range(lo, hi):
                hys[r][f, 1] = jnp.zeros((4, 512), F32)

    loads = [
        pltpu.make_async_copy(gas_hbm.at[pl.ds(3, 1)], g0.at[pl.ds(3, 1), pl.ds(1, 4)], in_sem.at[0]),
        pltpu.make_async_copy(gas_hbm.at[pl.ds(0, 3)], g0.at[pl.ds(0, 3), pl.ds(1, 4)], in_sem.at[1]),
        pltpu.make_async_copy(gas_hbm.at[pl.ds(4, 1)], g0.at[pl.ds(4, 1), pl.ds(1, 4)], in_sem.at[2]),
        pltpu.make_async_copy(cell_hbm, cell, in_sem.at[3]),
        pltpu.make_async_copy(state_hbm, state, in_sem.at[4]),
        pltpu.make_async_copy(slot_hbm, slot, in_sem.at[5]),
        pltpu.make_async_copy(dest_hbm, dest, in_sem.at[6]),
    ]
    barrier = pltpu.get_barrier_semaphore()
    for to in (below, above, left, right):
        pl.semaphore_signal(barrier, inc=1, device_id=to, device_id_type=pl.DeviceIdType.MESH)
    for load in loads:
        load.start()
    loads[0].wait()
    stage(0, 3)
    pl.semaphore_wait(barrier, 4)
    send(0, 0)
    loads[1].wait()
    for f in range(3):
        stage(0, f)
    send(0, 1)
    loads[2].wait()
    stage(0, 4)
    acc[...] = jnp.zeros_like(acc)
    rel[...] = jnp.zeros_like(rel)
    receive(0, 0)

    def first_heat(i, carry):
        g1[3, i] = plane(g0, hy0, 3, i)
        return carry
    lax.fori_loop(1, 5, first_heat, 0)
    stage(1, 3)
    send(1, 0)
    send(0, 2)

    receive(0, 1)

    def first_wind(n, carry):
        f, i = n // 4, n % 4 + 1
        fresh = plane(g0, hy0, f, i)
        g1[f, i] = fresh + jnp.where(f == 2, 0.1, 0.0) * g0[3, i]
        return carry
    lax.fori_loop(0, 12, first_wind, 0)
    for f in range(3):
        stage(1, f)
    send(1, 1)
    receive(1, 0)

    def second_heat(i, carry):
        t2[i - 1] = plane(g1, hy1, 3, i)
        return carry
    lax.fori_loop(1, 5, second_heat, 0)
    table(t2[...].reshape(128, 512), tab)
    loads[3].wait()
    steps = 128 // ROWS

    def gather(b, carry):
        gather_block(b, ROWS, cell, tab, seen)
        return carry
    lax.fori_loop(0, steps, gather, 0)
    loads[4].wait()
    burn_all(state, seen[...], state_out, rec)

    receive(0, 2)

    def first_fuel(i, carry):
        g1[4, i] = plane(g0, hy0, 4, i)
        return carry
    lax.fori_loop(1, 5, first_fuel, 0)
    stage(1, 4)
    send(1, 2)

    loads[5].wait()
    loads[6].wait()

    def compact(b, carry):
        compact_block(b, ROWS, slot, dest, rec, acc)
        return carry
    lax.fori_loop(0, steps, compact, 0)
    place = lax.broadcasted_iota(jnp.int32, (8, 256), 0) * 256 + lax.broadcasted_iota(jnp.int32, (8, 256), 1)
    for f in range(4):
        first, second = acc[32 * f:32 * f + 16, :], acc[32 * f + 16:32 * f + 32, :]
        both = first * 256.0 + second if f == 3 else first + second
        for face in range(2):
            live = place < counts_ref[0, face]
            box[face, f] = jnp.where(live, both[8 * face:8 * face + 8], 0.0)
    faces = [
        remote(box.at[0], got.at[1], fs.at[0], fr.at[0], below),
        remote(box.at[1], got.at[0], fs.at[1], fr.at[1], above),
    ]
    for copy in faces:
        copy.start()

    def deposit(b, carry):
        ds = pl.ds(pl.multiple_of(b * ROWS, 8), ROWS)
        burned = jnp.where(slot[ds, :] < 0, rec[2, ds, :], 0.0)
        deposit_block(dest[ds, :], burned, ROWS, rel)
        return carry
    lax.fori_loop(0, steps, deposit, 0)

    receive(1, 1)

    def second_wind(n, carry):
        f, i = n // 4, n % 4 + 1
        fresh = plane(g1, hy1, f, i)
        gas_out[f, i - 1] = fresh + jnp.where(f == 2, 0.1, 0.0) * g1[3, i]
        return carry
    lax.fori_loop(0, 12, second_wind, 0)
    receive(1, 2)

    def second_fuel(i, carry):
        gas_out[4, i - 1] = plane(g1, hy1, 4, i)
        return carry
    lax.fori_loop(1, 5, second_fuel, 0)

    for copy in faces:
        copy.wait_recv()

    @pl.when(p == 0)
    def _():
        got[0] = jnp.zeros((4, 8, 256), F32)

    @pl.when(p == np_ - 1)
    def _():
        got[1] = jnp.zeros((4, 8, 256), F32)

    for d in range(2):
        where_to = got[d, 3].astype(jnp.int32)
        burned = got[d, 2]
        deposit_block(
            jnp.concatenate([where_to[:, :128], where_to[:, 128:]], axis=0),
            jnp.concatenate([burned[:, :128], burned[:, 128:]], axis=0), 16, rel)
        for f in range(3):
            arr_out[f, pl.ds(d, 8, stride=4), :] = got[d, f, :, 0:128]
            arr_out[f, pl.ds(2 + d, 8, stride=4), :] = got[d, f, :, 128:256]
    both = rel[:256, :] + rel[256:, :]
    release = jnp.concatenate([both[:128], both[128:]], axis=1).reshape(4, 32, 512)
    gas_out[3] = t2[...] + 1.5 * release
    gas_out[4] = gas_out[4] + release
    for r in range(2):
        for k in range(3):
            for copy in halo(r, k):
                copy.wait_send()
    for copy in faces:
        copy.wait_send()


def on_device(gas, parcel_state, parcel_cell, parcel_dest, send_slot, face_counts):
    square = lambda a: a.reshape(128, 128)
    state = parcel_state.reshape(2, 128, 128).transpose(1, 0, 2).reshape(256, 128)
    vm = pl.BlockSpec(memory_space=pltpu.VMEM)
    hbm = pl.BlockSpec(memory_space=pltpu.HBM)
    i32 = lambda *s: pltpu.VMEM(s, jnp.int32)
    f32 = lambda *s: pltpu.VMEM(s, F32)
    dma = pltpu.SemaphoreType.DMA
    gas_out, out, arr = pl.pallas_call(
        step_kernel,
        out_shape=(
            jax.ShapeDtypeStruct(gas.shape, F32),
            jax.ShapeDtypeStruct((256, 128), F32),
            jax.ShapeDtypeStruct((3, 32, 128), F32),
        ),
        in_specs=[hbm] * 5 + [pl.BlockSpec(memory_space=pltpu.SMEM)],
        out_specs=(vm, vm, vm),
        scratch_shapes=[
            f32(5, 6, 32, 512), f32(5, 6, 32, 512), f32(4, 32, 512),
            f32(5, 2, 4, 512), f32(5, 2, 4, 512), f32(5, 2, 4, 512), f32(5, 2, 4, 512),
            i32(128, 128), i32(128, 128), i32(128, 128), f32(256, 128),
            pltpu.VMEM((256, 512), BF), f32(128, 128), f32(3, 128, 128), f32(128, 256), f32(512, 256),
            f32(2, 4, 8, 256), f32(2, 4, 8, 256),
            dma((7,)), dma((2, 3, 2)), dma((2, 3, 2)), dma((2, 3, 2)), dma((2, 3, 2)), dma((2,)), dma((2,)),
        ],
        compiler_params=pltpu.CompilerParams(vmem_limit_bytes=60 << 20, collective_id=0, has_side_effects=True),
        name="dust_step",
    )(gas, square(parcel_cell), square(parcel_dest), square(send_slot), state, face_counts.reshape(1, 2))
    parcels_out = out.reshape(128, 2, 128).transpose(1, 0, 2).reshape(2, 16384)
    arrivals = arr.reshape(3, 16, 2, 128).transpose(2, 0, 1, 3).reshape(2, 3, 2048)
    return (gas_out, parcels_out, arrivals)


def solution(mesh):
    in_specs = (
        P(None, "prop", "cross", None),
        P(None, ("prop", "cross")),
        P(("prop", "cross")),
        P(("prop", "cross")),
        P(("prop", "cross")),
        P("prop", "cross", None),
    )
    out_specs = (
        P(None, "prop", "cross", None),
        P(None, ("prop", "cross")),
        P(None, None, ("prop", "cross")),
    )
    return jax.shard_map(
        on_device, mesh=mesh, in_specs=in_specs, out_specs=out_specs, check_vma=False
    )
```

time: 390 us -> 44.8 us (0.11)
  the two profiles are of different devices: /device:TPU:7 before, /device:TPU:0 now
where the time goes in v2:
time: 44.8 us; the launch traced here: 44.7 us
  Pallas kernels  40.2 us (90%)
  local copies, waits for them, and re-layouts  3.83 us (9%)
  between operations  0.66 us (1%)
    pallas_call x1, Pallas kernels, on_device(): pl.pallas_call(step_kernel, out_shape=(jax.ShapeDtypeStruct(gas.shape, F3...  40.2 us
    unnamed x7, local copies, waits for them, and re-layouts  3.83 us

profile of v2, /device:TPU:0, one launch (start us, length us, event | category | flops | bytes accessed | tf_op | source)
XLA Modules:
  0.0 44.7 jit_solution(13297898870452627525)
XLA Ops:
  0.6 40.2 %dust_step.1 = (f32[5,4,32,512]{3,2,1,0:T(8,128)}, f32[256,128]{1,0:T(8,128)}, f32[3,32,128]{2,1,0:T(8,128)}) custom-call(f32[5,4,32,512]{3,2,1,0:T(8,128)} %gas_hbm.1, s32[128,128]{1,0:T(8,128)} %bitcast.21, s32[128,128]{1,0:T(8,128)} %bitcast.22, s32[128,128]{1,0:T(8,128)} %bitcast.23, f32[256,128]{1,0:T(8,128)} %bitcast.19, s32[1,2]{1,0:T(1,128)} %bitcast.25), custom_call_target="tpu_custom_call" | custom-call | tf_op jit(solution)/shard_map/dust_step/pallas_call | solution.py:353
  40.8 0.0 copy-start
  40.8 0.0 copy-start.1
  40.8 2.5 %copy.15 = f32[5,4,32,512]{3,2,1,0:T(8,128)} copy(f32[5,4,32,512]{3,2,1,0:T(8,128)} %get-tuple-element.12) | data formatting | bytes 2621440
  43.4 0.0 copy-done
  43.4 0.7 %copy.16 = f32[2,16384]{1,0:T(2,128)} copy(f32[2,16384]{1,0:T(2,128)S(1)} %bitcast.20) | data formatting | bytes 262144
  44.0 0.0 copy-done.1
  44.0 0.6 %copy.17 = f32[2,3,2048]{2,0,1:T(2,128)} copy(f32[2,3,2048]{2,0,1:T(2,128)S(1)} %bitcast.24) | data formatting | bytes 98304
Async XLA Ops:
  40.8 2.6 %copy-start = (f32[256,128]{1,0:T(8,128)S(1)}, f32[256,128]{1,0:T(8,128)}, u32[]{:S(2)}) copy-start(f32[256,128]{1,0:T(8,128)} %get-tuple-element.7) | copy-start | bytes 393220
  40.8 3.2 %copy-start.1 = (f32[3,32,128]{2,1,0:T(8,128)S(1)}, f32[3,32,128]{2,1,0:T(8,128)}, u32[]{:S(2)}) copy-start(f32[3,32,128]{2,1,0:T(8,128)} %get-tuple-element.8) | copy-start | bytes 147460

commit v3 on v2

--- a/solution.py
+++ b/solution.py
@@ -8,7 +8,7 @@
 
 F32 = jnp.float32
 BF = jnp.bfloat16
-ROWS = 16
+ROWS = 64
 NT = (((1,), (1,)), ((), ()))
 GROUPS = ((3, 4), (0, 3), (4, 5))
 
@@ -33,6 +33,11 @@
 
 def low_of(cell):
     return (cell & 255).astype(F32)
+
+
+def half_key(cell, half):
+    key = ((cell >> 8) & 1) * 64 + ((cell >> 9) & 63)
+    return jnp.where((cell >> 15) == half, key, -1).astype(F32)
 
 
 def table(T, tab_ref):
@@ -41,21 +46,21 @@
     tab_ref[...] = m.T.astype(BF)
 
 
-def gather_block(b, rows, cell_ref, tab_ref, seen_ref):
-    cell = cell_ref[pl.ds(pl.multiple_of(b * rows, 8), rows), :]
-    key = key_of(cell)
+def gather_block(cell, half, tab_ref):
+    rows = cell.shape[0]
+    key = half_key(cell, half)
     lo = low_of(cell)
-    it = iota_bf(256)
-    one = jnp.ones((256, 128), BF)
-    zero = jnp.zeros((256, 128), BF)
-    oh = jnp.concatenate([jnp.where(it == wide(key[i:i + 1], 256), one, zero) for i in range(rows)], axis=1)
-    res = jnp.dot(tab_ref[:, :256], oh, preferred_element_type=F32) + jnp.dot(tab_ref[:, 256:], oh, preferred_element_type=F32)
+    it = iota_bf(128)
+    one = jnp.ones((128, 128), BF)
+    zero = jnp.zeros((128, 128), BF)
+    oh = jnp.concatenate([jnp.where(it == wide(key[i:i + 1], 128), one, zero) for i in range(rows)], axis=1)
+    res = jnp.dot(tab_ref[...], jnp.concatenate([oh, oh], axis=0), preferred_element_type=F32)
     itf = lax.broadcasted_iota(jnp.int32, (256, 128), 0).astype(F32)
     out = []
     for i in range(rows):
         r = res[:, i * 128:(i + 1) * 128]
         out.append(jnp.sum(jnp.where(itf == lo[i:i + 1], r, 0.0), axis=0, keepdims=True))
-    seen_ref[pl.ds(pl.multiple_of(b * rows, 8), rows), :] = jnp.concatenate(out, axis=0)
+    return jnp.concatenate(out, axis=0)
 
 
 def burn_all(state_ref, seen, out_ref, rec_ref):
@@ -94,7 +99,7 @@
         As.append(jnp.concatenate([jnp.where(m, wide(v[i:i + 1], 16), z16) for v in vals], axis=0))
     A = jnp.concatenate(As, axis=1)
     B = jnp.concatenate(Bs, axis=1)
-    acc_ref[...] += lax.dot_general(A, B, NT, preferred_element_type=F32)
+    acc_ref[...] += lax.dot_general(B, A, NT, preferred_element_type=F32)
 
 
 def deposit_block(dest, burned, rows, acc_ref):
@@ -129,60 +134,58 @@
     return c - 0.05 * advect + 0.12 * laplace
 
 
-def step_kernel(gas_hbm, cell_hbm, dest_hbm, slot_hbm, state_hbm, counts_ref,
+def step_kernel(gas_hbm, cell_hbm, dest_hbm, slot_hbm, state_hbm, counts_hbm,
                 gas_out, state_out, arr_out,
-                g0, g1, t2, hy0, hy1, sy0, sy1, cell, dest, slot, state,
+                g0, g1, t2, hy0, hy1, sy0, sy1, cell, dest, slot, state, counts,
                 tab, seen, rec, acc, rel, box, got,
                 in_sem, xs, xr, ys, yr, fs, fr):
     p, c = lax.axis_index("prop"), lax.axis_index("cross")
     np_, nc = lax.axis_size("prop"), lax.axis_size("cross")
+    side = lax.rem(p, 2)
     below = {"prop": lax.rem(p + np_ - 1, np_)}
     above = {"prop": lax.rem(p + 1, np_)}
+    near = {"prop": p + 1 - 2 * side}
+    far = {"prop": lax.rem(p + np_ - 1 + 2 * side, np_)}
     left = {"cross": lax.rem(c + nc - 1, nc)}
     right = {"cross": lax.rem(c + 1, nc)}
+    near_half, far_half = 1 - side, side
+    edge = jnp.logical_or(p == 0, p == np_ - 1)
     gs, hys, sys_ = (g0, g1), (hy0, hy1), (sy0, sy1)
 
     def remote(a, b, s, r, to):
         return pltpu.make_async_remote_copy(src_ref=a, dst_ref=b, send_sem=s, recv_sem=r, device_id=to, device_id_type=pl.DeviceIdType.MESH)
 
-    def halo(r, k):
+    def halo_x(r, k, to_far):
         lo, hi = GROUPS[k]
         fields = pl.ds(lo, hi - lo)
-        if r == 0:
-            first, last = gas_hbm.at[fields, 0], gas_hbm.at[fields, 3]
-        else:
-            first, last = g1.at[fields, 1], g1.at[fields, 4]
-        sy, hy, g = sys_[r], hys[r], gs[r]
-        return [
-            remote(first, g.at[fields, 5], xs.at[r, k, 0], xr.at[r, k, 0], below),
-            remote(last, g.at[fields, 0], xs.at[r, k, 1], xr.at[r, k, 1], above),
+        source = 1 + 3 * side if to_far else 4 - 3 * side
+        first = gas_hbm.at[fields, source - 1] if r == 0 else g1.at[fields, source]
+        goal = 5 * (1 - side) if to_far else 5 * side
+        return remote(first, gs[r].at[fields, goal], xs.at[r, k, to_far], xr.at[r, k, to_far], far if to_far else near)
+
+    def halo_y(r, k):
+        lo, hi = GROUPS[k]
+        fields = pl.ds(lo, hi - lo)
+        sy, hy = sys_[r], hys[r]
+        return (
             remote(sy.at[fields, 0], hy.at[fields, 1], ys.at[r, k, 0], yr.at[r, k, 0], left),
             remote(sy.at[fields, 1], hy.at[fields, 0], ys.at[r, k, 1], yr.at[r, k, 1], right),
-        ]
+        )
 
     def stage(r, f):
         for i in range(4):
             sys_[r][f, 0, i:i + 1, :] = gs[r][f, 1 + i, 0:1, :]
             sys_[r][f, 1, i:i + 1, :] = gs[r][f, 1 + i, 31:32, :]
 
-    def send(r, k):
-        for copy in halo(r, k):
+    def send(copies):
+        for copy in copies:
             copy.start()
 
-    def receive(r, k):
-        for copy in halo(r, k):
+    def receive_near(r, k):
+        halo_x(r, k, 0).wait_recv()
+        for copy in halo_y(r, k):
             copy.wait_recv()
         lo, hi = GROUPS[k]
-
-        @pl.when(p == 0)
-        def _():
-            for f in range(lo, hi):
-                gs[r][f, 0] = jnp.zeros((32, 512), F32)
-
-        @pl.when(p == np_ - 1)
-        def _():
-            for f in range(lo, hi):
-                gs[r][f, 5] = jnp.zeros((32, 512), F32)
 
         @pl.when(c == 0)
         def _():
@@ -193,6 +196,15 @@
         def _():
             for f in range(lo, hi):
                 hys[r][f, 1] = jnp.zeros((4, 512), F32)
+
+    def receive_far(r, k):
+        halo_x(r, k, 1).wait_recv()
+        lo, hi = GROUPS[k]
+
+        @pl.when(edge)
+        def _():
+            for f in range(lo, hi):
+                gs[r][f, 5 * side] = jnp.zeros((32, 512), F32)
 
     loads = [
         pltpu.make_async_copy(gas_hbm.at[pl.ds(3, 1)], g0.at[pl.ds(3, 1), pl.ds(1, 4)], in_sem.at[0]),
@@ -202,91 +214,117 @@
         pltpu.make_async_copy(state_hbm, state, in_sem.at[4]),
         pltpu.make_async_copy(slot_hbm, slot, in_sem.at[5]),
         pltpu.make_async_copy(dest_hbm, dest, in_sem.at[6]),
+        pltpu.make_async_copy(counts_hbm, counts, in_sem.at[7]),
     ]
     barrier = pltpu.get_barrier_semaphore()
-    for to in (below, above, left, right):
+    for to in (near, far, left, right):
         pl.semaphore_signal(barrier, inc=1, device_id=to, device_id_type=pl.DeviceIdType.MESH)
-    for load in loads:
-        load.start()
+    send(loads)
     loads[0].wait()
     stage(0, 3)
     pl.semaphore_wait(barrier, 4)
-    send(0, 0)
+    send([halo_x(0, 0, 1), halo_x(0, 0, 0)])
+    send(halo_y(0, 0))
+    send([halo_x(0, 1, 1), halo_x(0, 1, 0)])
     loads[1].wait()
     for f in range(3):
         stage(0, f)
-    send(0, 1)
+    send(halo_y(0, 1))
     loads[2].wait()
     stage(0, 4)
+    send(halo_y(0, 2))
     acc[...] = jnp.zeros_like(acc)
     rel[...] = jnp.zeros_like(rel)
-    receive(0, 0)
+    receive_near(0, 0)
+    receive_far(0, 0)
 
     def first_heat(i, carry):
         g1[3, i] = plane(g0, hy0, 3, i)
         return carry
     lax.fori_loop(1, 5, first_heat, 0)
+    send([halo_x(1, 0, 1), halo_x(1, 0, 0)])
     stage(1, 3)
-    send(1, 0)
-    send(0, 2)
-
-    receive(0, 1)
-
-    def first_wind(n, carry):
-        f, i = n // 4, n % 4 + 1
-        fresh = plane(g0, hy0, f, i)
-        g1[f, i] = fresh + jnp.where(f == 2, 0.1, 0.0) * g0[3, i]
-        return carry
-    lax.fori_loop(0, 12, first_wind, 0)
+    send(halo_y(1, 0))
+    send([halo_x(0, 2, 1), halo_x(0, 2, 0)])
+
+    def first_wind(half):
+        def body(n, carry):
+            f, i = n // 2, n % 2 + 1 + 2 * half
+            fresh = plane(g0, hy0, f, i)
+            g1[f, i] = fresh + jnp.where(f == 2, 0.1, 0.0) * g0[3, i]
+            return carry
+        lax.fori_loop(0, 6, body, 0)
+
+    def first_fuel(half):
+        def body(n, carry):
+            i = n + 1 + 2 * half
+            g1[4, i] = plane(g0, hy0, 4, i)
+            return carry
+        lax.fori_loop(0, 2, body, 0)
+
+    def second_heat(half):
+        def body(n, carry):
+            i = n + 2 * half
+            t2[i] = plane(g1, hy1, 3, i + 1)
+            return carry
+        lax.fori_loop(0, 2, body, 0)
+        table(t2[pl.ds(2 * half, 2)].reshape(64, 512), tab)
+
+    receive_near(0, 1)
+    first_wind(near_half)
+    receive_near(0, 2)
+    first_fuel(near_half)
+    for load in loads[3:]:
+        load.wait()
+    receive_near(1, 0)
+    second_heat(near_half)
+    steps = 128 // ROWS
+
+    def near_gather(b, carry):
+        ds = pl.ds(pl.multiple_of(b * ROWS, 8), ROWS)
+        seen[ds, :] = gather_block(cell[ds, :], near_half, tab)
+        return carry
+    lax.fori_loop(0, steps, near_gather, 0)
+
+    receive_far(0, 1)
+    first_wind(far_half)
+    send([halo_x(1, 1, 1), halo_x(1, 1, 0)])
     for f in range(3):
         stage(1, f)
-    send(1, 1)
-    receive(1, 0)
-
-    def second_heat(i, carry):
-        t2[i - 1] = plane(g1, hy1, 3, i)
-        return carry
-    lax.fori_loop(1, 5, second_heat, 0)
-    table(t2[...].reshape(128, 512), tab)
-    loads[3].wait()
-    steps = 128 // ROWS
-
-    def gather(b, carry):
-        gather_block(b, ROWS, cell, tab, seen)
-        return carry
-    lax.fori_loop(0, steps, gather, 0)
-    loads[4].wait()
+    send(halo_y(1, 1))
+    receive_far(1, 0)
+    second_heat(far_half)
+
+    def far_gather(b, carry):
+        ds = pl.ds(pl.multiple_of(b * ROWS, 8), ROWS)
+        seen[ds, :] += gather_block(cell[ds, :], far_half, tab)
+        return carry
+    lax.fori_loop(0, steps, far_gather, 0)
     burn_all(state, seen[...], state_out, rec)
 
-    receive(0, 2)
-
-    def first_fuel(i, carry):
-        g1[4, i] = plane(g0, hy0, 4, i)
-        return carry
-    lax.fori_loop(1, 5, first_fuel, 0)
+    receive_far(0, 2)
+    first_fuel(far_half)
+    send([halo_x(1, 2, 1), halo_x(1, 2, 0)])
     stage(1, 4)
-    send(1, 2)
-
-    loads[5].wait()
-    loads[6].wait()
+    send(halo_y(1, 2))
 
     def compact(b, carry):
         compact_block(b, ROWS, slot, dest, rec, acc)
         return carry
     lax.fori_loop(0, steps, compact, 0)
     place = lax.broadcasted_iota(jnp.int32, (8, 256), 0) * 256 + lax.broadcasted_iota(jnp.int32, (8, 256), 1)
+    turned = acc[...].T
     for f in range(4):
-        first, second = acc[32 * f:32 * f + 16, :], acc[32 * f + 16:32 * f + 32, :]
+        first, second = turned[32 * f:32 * f + 16, :], turned[32 * f + 16:32 * f + 32, :]
         both = first * 256.0 + second if f == 3 else first + second
         for face in range(2):
-            live = place < counts_ref[0, face]
+            live = place < counts[0, face]
             box[face, f] = jnp.where(live, both[8 * face:8 * face + 8], 0.0)
     faces = [
         remote(box.at[0], got.at[1], fs.at[0], fr.at[0], below),
         remote(box.at[1], got.at[0], fs.at[1], fr.at[1], above),
     ]
-    for copy in faces:
-        copy.start()
+    send(faces)
 
     def deposit(b, carry):
         ds = pl.ds(pl.multiple_of(b * ROWS, 8), ROWS)
@@ -295,7 +333,8 @@
         return carry
     lax.fori_loop(0, steps, deposit, 0)
 
-    receive(1, 1)
+    receive_near(1, 1)
+    receive_far(1, 1)
 
     def second_wind(n, carry):
         f, i = n // 4, n % 4 + 1
@@ -303,7 +342,8 @@
         gas_out[f, i - 1] = fresh + jnp.where(f == 2, 0.1, 0.0) * g1[3, i]
         return carry
     lax.fori_loop(0, 12, second_wind, 0)
-    receive(1, 2)
+    receive_near(1, 2)
+    receive_far(1, 2)
 
     def second_fuel(i, carry):
         gas_out[4, i - 1] = plane(g1, hy1, 4, i)
@@ -321,22 +361,22 @@
     def _():
         got[1] = jnp.zeros((4, 8, 256), F32)
 
+    where_to, burned = [], []
     for d in range(2):
-        where_to = got[d, 3].astype(jnp.int32)
-        burned = got[d, 2]
-        deposit_block(
-            jnp.concatenate([where_to[:, :128], where_to[:, 128:]], axis=0),
-            jnp.concatenate([burned[:, :128], burned[:, 128:]], axis=0), 16, rel)
-        for f in range(3):
-            arr_out[f, pl.ds(d, 8, stride=4), :] = got[d, f, :, 0:128]
-            arr_out[f, pl.ds(2 + d, 8, stride=4), :] = got[d, f, :, 128:256]
+        for part in range(2):
+            lanes = slice(128 * part, 128 * part + 128)
+            where_to.append(got[d, 3, :, lanes].astype(jnp.int32))
+            burned.append(got[d, 2, :, lanes])
+            for f in range(3):
+                arr_out[f, pl.ds(2 * part + d, 8, stride=4), :] = got[d, f, :, lanes]
+    deposit_block(jnp.concatenate(where_to, axis=0), jnp.concatenate(burned, axis=0), 32, rel)
     both = rel[:256, :] + rel[256:, :]
     release = jnp.concatenate([both[:128], both[128:]], axis=1).reshape(4, 32, 512)
     gas_out[3] = t2[...] + 1.5 * release
     gas_out[4] = gas_out[4] + release
     for r in range(2):
         for k in range(3):
-            for copy in halo(r, k):
+            for copy in (halo_x(r, k, 0), halo_x(r, k, 1)) + halo_y(r, k):
                 copy.wait_send()
     for copy in faces:
         copy.wait_send()
@@ -350,6 +390,7 @@
     i32 = lambda *s: pltpu.VMEM(s, jnp.int32)
     f32 = lambda *s: pltpu.VMEM(s, F32)
     dma = pltpu.SemaphoreType.DMA
+    inputs = (gas, square(parcel_cell), square(parcel_dest), square(send_slot), state, face_counts.reshape(1, 2))
     gas_out, out, arr = pl.pallas_call(
         step_kernel,
         out_shape=(
@@ -357,19 +398,19 @@
             jax.ShapeDtypeStruct((256, 128), F32),
             jax.ShapeDtypeStruct((3, 32, 128), F32),
         ),
-        in_specs=[hbm] * 5 + [pl.BlockSpec(memory_space=pltpu.SMEM)],
+        in_specs=[hbm] * 6,
         out_specs=(vm, vm, vm),
         scratch_shapes=[
             f32(5, 6, 32, 512), f32(5, 6, 32, 512), f32(4, 32, 512),
             f32(5, 2, 4, 512), f32(5, 2, 4, 512), f32(5, 2, 4, 512), f32(5, 2, 4, 512),
-            i32(128, 128), i32(128, 128), i32(128, 128), f32(256, 128),
-            pltpu.VMEM((256, 512), BF), f32(128, 128), f32(3, 128, 128), f32(128, 256), f32(512, 256),
+            i32(128, 128), i32(128, 128), i32(128, 128), f32(256, 128), pltpu.SMEM((1, 2), jnp.int32),
+            pltpu.VMEM((256, 256), BF), f32(128, 128), f32(3, 128, 128), f32(256, 128), f32(512, 256),
             f32(2, 4, 8, 256), f32(2, 4, 8, 256),
-            dma((7,)), dma((2, 3, 2)), dma((2, 3, 2)), dma((2, 3, 2)), dma((2, 3, 2)), dma((2,)), dma((2,)),
+            dma((8,)), dma((2, 3, 2)), dma((2, 3, 2)), dma((2, 3, 2)), dma((2, 3, 2)), dma((2,)), dma((2,)),
         ],
-        compiler_params=pltpu.CompilerParams(vmem_limit_bytes=60 << 20, collective_id=0, has_side_effects=True),
+        compiler_params=pltpu.CompilerParams(vmem_limit_bytes=44 << 20, collective_id=0, has_side_effects=True),
         name="dust_step",
-    )(gas, square(parcel_cell), square(parcel_dest), square(send_slot), state, face_counts.reshape(1, 2))
+    )(*[pltpu.with_memory_space_constraint(a, pltpu.HBM) for a in inputs])
     parcels_out = out.reshape(128, 2, 128).transpose(1, 0, 2).reshape(2, 16384)
     arrivals = arr.reshape(3, 16, 2, 128).transpose(2, 0, 1, 3).reshape(2, 3, 2048)
     return (gas_out, parcels_out, arrivals)

time: 44.8 us -> 38 us (0.85)
  Pallas kernels: 40.2 us -> 34.9 us
  local copies, waits for them, and re-layouts: 3.83 us -> 2.33 us
    pallas_call x1, Pallas kernels: 40.2 us -> 34.9 us  [on_device(): pl.pallas_call(step_kernel, out_shape=(jax.ShapeDtypeStruct(gas.shape, F3...]
    unnamed x7 -> x3, local copies, waits for them, and re-layouts: 3.83 us -> 2.33 us
where the time goes in v3:
time: 38 us; the launch traced here: 37.9 us
  Pallas kernels  34.9 us (92%)
  local copies, waits for them, and re-layouts  2.33 us (6%)
  between operations  0.64 us (2%)
    pallas_call x1, Pallas kernels, on_device(): pl.pallas_call(step_kernel, out_shape=(jax.ShapeDtypeStruct(gas.shape, F3...  34.9 us
    unnamed x3, local copies, waits for them, and re-layouts  2.33 us

profile of v3, /device:TPU:0, one launch (start us, length us, event | category | flops | bytes accessed | tf_op | source)
XLA Modules:
  0.0 37.9 jit_solution(17192196453341973689)
XLA Ops:
  0.6 34.9 %dust_step.1 = (f32[5,4,32,512]{3,2,1,0:T(8,128)S(1)}, f32[256,128]{1,0:T(8,128)S(1)}, f32[3,32,128]{2,1,0:T(8,128)S(1)}) custom-call(f32[5,4,32,512]{3,2,1,0:T(8,128)} %gas_hbm.1, s32[128,128]{1,0:T(8,128)} %bitcast.22, s32[128,128]{1,0:T(8,128)} %bitcast.23, s32[128,128]{1,0:T(8,128)} %bitcast.24, f32[256,128]{1,0:T(8,128)} %bitcast.21, s32[1,2]{1,0:T(1,128)} %bitcast.25), custom_call_target="tpu_custom_call" | custom-call | tf_op jit(solution)/shard_map/dust_step/pallas_call | solution.py:394
  35.6 1.1 %copy.15 = f32[5,4,32,512]{3,2,1,0:T(8,128)} copy(f32[5,4,32,512]{3,2,1,0:T(8,128)S(1)} %get-tuple-element.12) | data formatting | bytes 2621440
  36.6 0.7 %copy.16 = f32[2,16384]{1,0:T(2,128)} copy(f32[2,16384]{1,0:T(2,128)S(1)} %bitcast.19) | data formatting | bytes 262144
  37.3 0.6 %copy.17 = f32[2,3,2048]{2,0,1:T(2,128)} copy(f32[2,3,2048]{2,0,1:T(2,128)S(1)} %bitcast.20) | data formatting | bytes 98304

commit v4 on v3

--- a/solution.py
+++ b/solution.py
@@ -122,23 +122,25 @@
 def plane(g, hy, f, i):
     c = g[f, i]
     rows, depth = c.shape
-    row = lax.broadcasted_iota(jnp.int32, (rows, depth), 0)
-    lane = lax.broadcasted_iota(jnp.int32, (rows, depth), 1)
+    row = lax.broadcasted_iota(jnp.int32, (8, depth), 0)
+    lane = lax.broadcasted_iota(jnp.int32, (rows, 128), 1)
     xm, xp = g[f, i - 1], g[f, i + 1]
-    ym = jnp.where(row == 0, hy[f, 0, pl.ds(i - 1, 1), :], pltpu.roll(c, 1, 0))
-    yp = jnp.where(row == rows - 1, hy[f, 1, pl.ds(i - 1, 1), :], pltpu.roll(c, rows - 1, 0))
-    zm = jnp.where(lane == 0, 0.0, pltpu.roll(c, 1, 1))
-    zp = jnp.where(lane == depth - 1, 0.0, pltpu.roll(c, depth - 1, 1))
+    down, up = pltpu.roll(c, 1, 0), pltpu.roll(c, rows - 1, 0)
+    ym = jnp.concatenate([jnp.where(row == 0, hy[f, 0, pl.ds(i - 1, 1), :], down[:8]), down[8:]], axis=0)
+    yp = jnp.concatenate([up[:-8], jnp.where(row == 7, hy[f, 1, pl.ds(i - 1, 1), :], up[-8:])], axis=0)
+    back, on = pltpu.roll(c, 1, 1), pltpu.roll(c, depth - 1, 1)
+    zm = jnp.concatenate([jnp.where(lane == 0, 0.0, back[:, :128]), back[:, 128:]], axis=1)
+    zp = jnp.concatenate([on[:, :-128], jnp.where(lane == 127, 0.0, on[:, -128:])], axis=1)
     advect = g[0, i] * (xp - xm) + g[1, i] * (yp - ym) + g[2, i] * (zp - zm)
-    laplace = (xp + xm) + (yp + ym) + (zp + zm) - 6.0 * c
-    return c - 0.05 * advect + 0.12 * laplace
+    around = (xp + xm) + (yp + ym) + (zp + zm)
+    return (0.28 * c + 0.12 * around) - 0.05 * advect
 
 
 def step_kernel(gas_hbm, cell_hbm, dest_hbm, slot_hbm, state_hbm, counts_hbm,
                 gas_out, state_out, arr_out,
                 g0, g1, t2, hy0, hy1, sy0, sy1, cell, dest, slot, state, counts,
                 tab, seen, rec, acc, rel, box, got,
-                in_sem, xs, xr, ys, yr, fs, fr):
+                in_sem, fars, farr, xs, xr, ys, yr, fs, fr):
     p, c = lax.axis_index("prop"), lax.axis_index("cross")
     np_, nc = lax.axis_size("prop"), lax.axis_size("cross")
     side = lax.rem(p, 2)
@@ -149,62 +151,86 @@
     left = {"cross": lax.rem(c + nc - 1, nc)}
     right = {"cross": lax.rem(c + 1, nc)}
     near_half, far_half = 1 - side, side
+    inner, outer, rest = 4 - 3 * side, 1 + 3 * side, 2 - side
+    has_below, has_above, has_left, has_right = p > 0, p < np_ - 1, c > 0, c < nc - 1
     edge = jnp.logical_or(p == 0, p == np_ - 1)
+    has_far = jnp.logical_not(edge)
     gs, hys, sys_ = (g0, g1), (hy0, hy1), (sy0, sy1)
 
     def remote(a, b, s, r, to):
         return pltpu.make_async_remote_copy(src_ref=a, dst_ref=b, send_sem=s, recv_sem=r, device_id=to, device_id_type=pl.DeviceIdType.MESH)
 
-    def halo_x(r, k, to_far):
+    def halo_far(r, f):
+        source = gas_hbm.at[f, outer - 1] if r == 0 else g1.at[f, outer]
+        return remote(source, gs[r].at[f, 5 * (1 - side)], fars.at[r, f], farr.at[r, f], far)
+
+    def halo_near(r, k):
         lo, hi = GROUPS[k]
         fields = pl.ds(lo, hi - lo)
-        source = 1 + 3 * side if to_far else 4 - 3 * side
-        first = gas_hbm.at[fields, source - 1] if r == 0 else g1.at[fields, source]
-        goal = 5 * (1 - side) if to_far else 5 * side
-        return remote(first, gs[r].at[fields, goal], xs.at[r, k, to_far], xr.at[r, k, to_far], far if to_far else near)
-
-    def halo_y(r, k):
+        source = gas_hbm.at[fields, inner - 1] if r == 0 else g1.at[fields, inner]
+        return remote(source, gs[r].at[fields, 5 * side], xs.at[r, k], xr.at[r, k], near)
+
+    def halo_y(r, k, d):
         lo, hi = GROUPS[k]
         fields = pl.ds(lo, hi - lo)
-        sy, hy = sys_[r], hys[r]
-        return (
-            remote(sy.at[fields, 0], hy.at[fields, 1], ys.at[r, k, 0], yr.at[r, k, 0], left),
-            remote(sy.at[fields, 1], hy.at[fields, 0], ys.at[r, k, 1], yr.at[r, k, 1], right),
-        )
-
-    def stage(r, f):
-        for i in range(4):
-            sys_[r][f, 0, i:i + 1, :] = gs[r][f, 1 + i, 0:1, :]
-            sys_[r][f, 1, i:i + 1, :] = gs[r][f, 1 + i, 31:32, :]
-
-    def send(copies):
-        for copy in copies:
-            copy.start()
+        return remote(sys_[r].at[fields, d], hys[r].at[fields, 1 - d], ys.at[r, k, d], yr.at[r, k, d], right if d else left)
+
+    def stage(r, k):
+        for f in range(*GROUPS[k]):
+            for i in range(4):
+                sys_[r][f, 0, i:i + 1, :] = gs[r][f, 1 + i, 0:1, :]
+                sys_[r][f, 1, i:i + 1, :] = gs[r][f, 1 + i, 31:32, :]
+
+    def send_far(r, *fields):
+        @pl.when(has_far)
+        def _():
+            for f in fields:
+                halo_far(r, f).start()
+
+    def send_near(r, k):
+        halo_near(r, k).start()
+
+    def send_y(r, *groups):
+        @pl.when(has_left)
+        def _():
+            for k in groups:
+                halo_y(r, k, 0).start()
+
+        @pl.when(has_right)
+        def _():
+            for k in groups:
+                halo_y(r, k, 1).start()
 
     def receive_near(r, k):
-        halo_x(r, k, 0).wait_recv()
-        for copy in halo_y(r, k):
-            copy.wait_recv()
-        lo, hi = GROUPS[k]
-
-        @pl.when(c == 0)
-        def _():
-            for f in range(lo, hi):
-                hys[r][f, 0] = jnp.zeros((4, 512), F32)
-
-        @pl.when(c == nc - 1)
-        def _():
-            for f in range(lo, hi):
-                hys[r][f, 1] = jnp.zeros((4, 512), F32)
-
-    def receive_far(r, k):
-        halo_x(r, k, 1).wait_recv()
-        lo, hi = GROUPS[k]
-
-        @pl.when(edge)
-        def _():
-            for f in range(lo, hi):
-                gs[r][f, 5 * side] = jnp.zeros((32, 512), F32)
+        halo_near(r, k).wait_recv()
+
+        @pl.when(has_left)
+        def _():
+            halo_y(r, k, 1).wait_recv()
+
+        @pl.when(has_right)
+        def _():
+            halo_y(r, k, 0).wait_recv()
+
+    def receive_far(r, *fields):
+        @pl.when(has_far)
+        def _():
+            for f in fields:
+                halo_far(r, f).wait_recv()
+
+    def first(f, i):
+        fresh = plane(g0, hy0, f, i)
+        g1[f, i] = fresh + 0.1 * g0[3, i] if f == 2 else fresh
+
+    def second(f, i):
+        fresh = plane(g1, hy1, f, i)
+        gas_out[f, i - 1] = fresh + 0.1 * g1[3, i] if f == 2 else fresh
+
+    def on_rest(todo):
+        def body(n, carry):
+            todo(rest + n)
+            return carry
+        lax.fori_loop(0, 3, body, 0)
 
     loads = [
         pltpu.make_async_copy(gas_hbm.at[pl.ds(3, 1)], g0.at[pl.ds(3, 1), pl.ds(1, 4)], in_sem.at[0]),
@@ -217,50 +243,77 @@
         pltpu.make_async_copy(counts_hbm, counts, in_sem.at[7]),
     ]
     barrier = pltpu.get_barrier_semaphore()
-    for to in (near, far, left, right):
+    def greet(to):
         pl.semaphore_signal(barrier, inc=1, device_id=to, device_id_type=pl.DeviceIdType.MESH)
-    send(loads)
+
+    greet(near)
+    pl.when(has_far)(lambda: greet(far))
+    pl.when(has_left)(lambda: greet(left))
+    pl.when(has_right)(lambda: greet(right))
+    for load in loads:
+        load.start()
+
+    @pl.when(edge)
+    def _():
+        for g in gs:
+            for f in range(5):
+                g[f, 5 * side] = jnp.zeros((32, 512), F32)
+
+    @pl.when(c == 0)
+    def _():
+        for hy in hys:
+            hy[:, 0] = jnp.zeros((5, 4, 512), F32)
+
+    @pl.when(c == nc - 1)
+    def _():
+        for hy in hys:
+            hy[:, 1] = jnp.zeros((5, 4, 512), F32)
+
+    @pl.when(p == 0)
+    def _():
+        got[0] = jnp.zeros((4, 8, 256), F32)
+
+    @pl.when(p == np_ - 1)
+    def _():
+        got[1] = jnp.zeros((4, 8, 256), F32)
+
     loads[0].wait()
-    stage(0, 3)
-    pl.semaphore_wait(barrier, 4)
-    send([halo_x(0, 0, 1), halo_x(0, 0, 0)])
-    send(halo_y(0, 0))
-    send([halo_x(0, 1, 1), halo_x(0, 1, 0)])
+    stage(0, 0)
     loads[1].wait()
-    for f in range(3):
-        stage(0, f)
-    send(halo_y(0, 1))
+    stage(0, 1)
     loads[2].wait()
-    stage(0, 4)
-    send(halo_y(0, 2))
+    stage(0, 2)
+    pl.semaphore_wait(barrier, 1 + has_far.astype(jnp.int32) + has_left.astype(jnp.int32) + has_right.astype(jnp.int32))
+    send_y(0, 0)
+    send_far(0, 3)
+    send_near(0, 0)
+    send_y(0, 1, 2)
+    send_far(0, 0, 1)
+    send_near(0, 1)
+    send_near(0, 2)
     acc[...] = jnp.zeros_like(acc)
     rel[...] = jnp.zeros_like(rel)
+
     receive_near(0, 0)
-    receive_far(0, 0)
-
-    def first_heat(i, carry):
-        g1[3, i] = plane(g0, hy0, 3, i)
-        return carry
-    lax.fori_loop(1, 5, first_heat, 0)
-    send([halo_x(1, 0, 1), halo_x(1, 0, 0)])
-    stage(1, 3)
-    send(halo_y(1, 0))
-    send([halo_x(0, 2, 1), halo_x(0, 2, 0)])
-
-    def first_wind(half):
-        def body(n, carry):
-            f, i = n // 2, n % 2 + 1 + 2 * half
-            fresh = plane(g0, hy0, f, i)
-            g1[f, i] = fresh + jnp.where(f == 2, 0.1, 0.0) * g0[3, i]
-            return carry
-        lax.fori_loop(0, 6, body, 0)
-
-    def first_fuel(half):
-        def body(n, carry):
-            i = n + 1 + 2 * half
-            g1[4, i] = plane(g0, hy0, 4, i)
-            return carry
-        lax.fori_loop(0, 2, body, 0)
+    on_rest(lambda i: first(3, i))
+    receive_far(0, 3)
+    first(3, outer)
+    stage(1, 0)
+    send_y(1, 0)
+    send_near(1, 0)
+    send_far(0, 2)
+    send_far(1, 3)
+    send_far(0, 4)
+    receive_near(0, 1)
+
+    def winds(i):
+        for f in range(3):
+            first(f, i)
+    on_rest(winds)
+    receive_near(0, 2)
+    on_rest(lambda i: first(4, i))
+    for load in loads[3:]:
+        load.wait()
 
     def second_heat(half):
         def body(n, carry):
@@ -270,97 +323,71 @@
         lax.fori_loop(0, 2, body, 0)
         table(t2[pl.ds(2 * half, 2)].reshape(64, 512), tab)
 
-    receive_near(0, 1)
-    first_wind(near_half)
-    receive_near(0, 2)
-    first_fuel(near_half)
-    for load in loads[3:]:
-        load.wait()
+    def on_blocks(todo):
+        def body(b, carry):
+            todo(b, pl.ds(pl.multiple_of(b * ROWS, 8), ROWS))
+            return carry
+        lax.fori_loop(0, 128 // ROWS, body, 0)
+
     receive_near(1, 0)
     second_heat(near_half)
-    steps = 128 // ROWS
-
-    def near_gather(b, carry):
-        ds = pl.ds(pl.multiple_of(b * ROWS, 8), ROWS)
+
+    def near_gather(b, ds):
         seen[ds, :] = gather_block(cell[ds, :], near_half, tab)
-        return carry
-    lax.fori_loop(0, steps, near_gather, 0)
-
-    receive_far(0, 1)
-    first_wind(far_half)
-    send([halo_x(1, 1, 1), halo_x(1, 1, 0)])
-    for f in range(3):
-        stage(1, f)
-    send(halo_y(1, 1))
-    receive_far(1, 0)
+    on_blocks(near_gather)
+
+    receive_far(0, 0, 1, 2)
+    winds(outer)
+    stage(1, 1)
+    send_y(1, 1)
+    send_far(1, 0, 1, 2)
+    send_near(1, 1)
+    receive_far(1, 3)
     second_heat(far_half)
 
-    def far_gather(b, carry):
-        ds = pl.ds(pl.multiple_of(b * ROWS, 8), ROWS)
+    def far_gather(b, ds):
         seen[ds, :] += gather_block(cell[ds, :], far_half, tab)
-        return carry
-    lax.fori_loop(0, steps, far_gather, 0)
+    on_blocks(far_gather)
+    receive_far(0, 4)
+    first(4, outer)
+    stage(1, 2)
+    send_y(1, 2)
+    send_far(1, 4)
+    send_near(1, 2)
     burn_all(state, seen[...], state_out, rec)
-
-    receive_far(0, 2)
-    first_fuel(far_half)
-    send([halo_x(1, 2, 1), halo_x(1, 2, 0)])
-    stage(1, 4)
-    send(halo_y(1, 2))
-
-    def compact(b, carry):
-        compact_block(b, ROWS, slot, dest, rec, acc)
-        return carry
-    lax.fori_loop(0, steps, compact, 0)
+    on_blocks(lambda b, ds: compact_block(b, ROWS, slot, dest, rec, acc))
     place = lax.broadcasted_iota(jnp.int32, (8, 256), 0) * 256 + lax.broadcasted_iota(jnp.int32, (8, 256), 1)
     turned = acc[...].T
     for f in range(4):
-        first, second = turned[32 * f:32 * f + 16, :], turned[32 * f + 16:32 * f + 32, :]
-        both = first * 256.0 + second if f == 3 else first + second
+        head, tail = turned[32 * f:32 * f + 16, :], turned[32 * f + 16:32 * f + 32, :]
+        both = head * 256.0 + tail if f == 3 else head + tail
         for face in range(2):
             live = place < counts[0, face]
             box[face, f] = jnp.where(live, both[8 * face:8 * face + 8], 0.0)
-    faces = [
-        remote(box.at[0], got.at[1], fs.at[0], fr.at[0], below),
-        remote(box.at[1], got.at[0], fs.at[1], fr.at[1], above),
-    ]
-    send(faces)
-
-    def deposit(b, carry):
-        ds = pl.ds(pl.multiple_of(b * ROWS, 8), ROWS)
+    down = remote(box.at[0], got.at[1], fs.at[0], fr.at[0], below)
+    up = remote(box.at[1], got.at[0], fs.at[1], fr.at[1], above)
+    pl.when(has_below)(down.start)
+    pl.when(has_above)(up.start)
+
+    def deposit(b, ds):
         burned = jnp.where(slot[ds, :] < 0, rec[2, ds, :], 0.0)
         deposit_block(dest[ds, :], burned, ROWS, rel)
-        return carry
-    lax.fori_loop(0, steps, deposit, 0)
+    on_blocks(deposit)
 
     receive_near(1, 1)
-    receive_far(1, 1)
-
-    def second_wind(n, carry):
-        f, i = n // 4, n % 4 + 1
-        fresh = plane(g1, hy1, f, i)
-        gas_out[f, i - 1] = fresh + jnp.where(f == 2, 0.1, 0.0) * g1[3, i]
-        return carry
-    lax.fori_loop(0, 12, second_wind, 0)
+
+    def later_winds(i):
+        for f in range(3):
+            second(f, i)
+    on_rest(later_winds)
     receive_near(1, 2)
-    receive_far(1, 2)
-
-    def second_fuel(i, carry):
-        gas_out[4, i - 1] = plane(g1, hy1, 4, i)
-        return carry
-    lax.fori_loop(1, 5, second_fuel, 0)
-
-    for copy in faces:
-        copy.wait_recv()
-
-    @pl.when(p == 0)
-    def _():
-        got[0] = jnp.zeros((4, 8, 256), F32)
-
-    @pl.when(p == np_ - 1)
-    def _():
-        got[1] = jnp.zeros((4, 8, 256), F32)
-
+    on_rest(lambda i: second(4, i))
+    for f in (0, 1, 2, 4):
+        receive_far(1, f)
+        second(f, outer)
+
+    pl.when(has_below)(up.wait_recv)
+    pl.when(has_above)(down.wait_recv)
     where_to, burned = [], []
     for d in range(2):
         for part in range(2):
@@ -374,12 +401,24 @@
     release = jnp.concatenate([both[:128], both[128:]], axis=1).reshape(4, 32, 512)
     gas_out[3] = t2[...] + 1.5 * release
     gas_out[4] = gas_out[4] + release
+
+    @pl.when(has_far)
+    def _():
+        for r in range(2):
+            for f in range(5):
+                halo_far(r, f).wait_send()
+
     for r in range(2):
         for k in range(3):
-            for copy in (halo_x(r, k, 0), halo_x(r, k, 1)) + halo_y(r, k):
-                copy.wait_send()
-    for copy in faces:
-        copy.wait_send()
+            halo_near(r, k).wait_send()
+    for d, there in ((0, has_left), (1, has_right)):
+        @pl.when(there)
+        def _():
+            for r in range(2):
+                for k in range(3):
+                    halo_y(r, k, d).wait_send()
+    pl.when(has_below)(down.wait_send)
+    pl.when(has_above)(up.wait_send)
 
 
 def on_device(gas, parcel_state, parcel_cell, parcel_dest, send_slot, face_counts):
@@ -406,7 +445,7 @@
             i32(128, 128), i32(128, 128), i32(128, 128), f32(256, 128), pltpu.SMEM((1, 2), jnp.int32),
             pltpu.VMEM((256, 256), BF), f32(128, 128), f32(3, 128, 128), f32(256, 128), f32(512, 256),
             f32(2, 4, 8, 256), f32(2, 4, 8, 256),
-            dma((8,)), dma((2, 3, 2)), dma((2, 3, 2)), dma((2, 3, 2)), dma((2, 3, 2)), dma((2,)), dma((2,)),
+            dma((8,)), dma((2, 5)), dma((2, 5)), dma((2, 3)), dma((2, 3)), dma((2, 3, 2)), dma((2, 3, 2)), dma((2,)), dma((2,)),
         ],
         compiler_params=pltpu.CompilerParams(vmem_limit_bytes=44 << 20, collective_id=0, has_side_effects=True),
         name="dust_step",

time: 38 us -> 32.8 us (0.86)
  the two profiles are of different devices: /device:TPU:0 before, /device:TPU:99 now
where the time goes in v4:
time: 32.8 us; the launch traced here: 32.7 us
  Pallas kernels  29.7 us (91%)
  local copies, waits for them, and re-layouts  2.33 us (7%)
  between operations  0.64 us (2%)
    pallas_call x1, Pallas kernels, on_device(): pl.pallas_call(step_kernel, out_shape=(jax.ShapeDtypeStruct(gas.shape, F3...  29.7 us
    unnamed x3, local copies, waits for them, and re-layouts  2.33 us

profile of v4, /device:TPU:99, one launch (start us, length us, event | category | flops | bytes accessed | tf_op | source)
XLA Modules:
  0.0 32.7 jit_solution(11056753125039056405)
XLA Ops:
  0.6 29.7 %dust_step.1 = (f32[5,4,32,512]{3,2,1,0:T(8,128)S(1)}, f32[256,128]{1,0:T(8,128)S(1)}, f32[3,32,128]{2,1,0:T(8,128)S(1)}) custom-call(f32[5,4,32,512]{3,2,1,0:T(8,128)} %gas_hbm.1, s32[128,128]{1,0:T(8,128)} %bitcast.22, s32[128,128]{1,0:T(8,128)} %bitcast.23, s32[128,128]{1,0:T(8,128)} %bitcast.24, f32[256,128]{1,0:T(8,128)} %bitcast.21, s32[1,2]{1,0:T(1,128)} %bitcast.25), custom_call_target="tpu_custom_call" | custom-call | tf_op jit(solution)/shard_map/dust_step/pallas_call | solution.py:433
  30.3 1.1 %copy.15 = f32[5,4,32,512]{3,2,1,0:T(8,128)} copy(f32[5,4,32,512]{3,2,1,0:T(8,128)S(1)} %get-tuple-element.12) | data formatting | bytes 2621440
  31.4 0.7 %copy.16 = f32[2,16384]{1,0:T(2,128)} copy(f32[2,16384]{1,0:T(2,128)S(1)} %bitcast.19) | data formatting | bytes 262144
  32.0 0.6 %copy.17 = f32[2,3,2048]{2,0,1:T(2,128)} copy(f32[2,3,2048]{2,0,1:T(2,128)S(1)} %bitcast.20) | data formatting | bytes 98304

commit v5 on v4

--- a/solution.py
+++ b/solution.py
@@ -63,30 +63,18 @@
     return jnp.concatenate(out, axis=0)
 
 
-def burn_all(state_ref, seen, out_ref, rec_ref):
-    mass = state_ref[pl.ds(0, 128, stride=2), :]
-    temper = state_ref[pl.ds(1, 128, stride=2), :]
+def burn(mass, temper, seen):
     hot = temper + 0.3 * (seen - temper)
     burned = 0.2 * mass * (1.0 + 0.5 * jnp.tanh(hot))
-    left = mass - burned
-    warm = hot + 0.5 * burned
-    out_ref[pl.ds(0, 128, stride=2), :] = left
-    out_ref[pl.ds(1, 128, stride=2), :] = warm
-    rec_ref[0] = left
-    rec_ref[1] = warm
-    rec_ref[2] = burned
-
-
-def compact_block(b, rows, slot_ref, dest_ref, rec_ref, acc_ref):
-    ds = pl.ds(pl.multiple_of(b * rows, 8), rows)
-    slot = slot_ref[ds, :]
-    dest = dest_ref[ds, :]
+    return mass - burned, hot + 0.5 * burned, burned
+
+
+def compact_block(b, rows, slot, dest, cell, mass, temper, acc_ref):
     hi = (slot >> 8).astype(F32)
     lo = (slot & 255).astype(F32)
-    vals = []
-    for f in range(3):
-        vals += list(split(rec_ref[f, ds, :]))
-    vals += [(dest >> 8).astype(F32), (dest & 255).astype(F32)]
+    vals = [*split(mass), *split(temper)]
+    for index in (cell, dest):
+        vals += [(index >> 8).astype(F32), (index & 255).astype(F32)]
     it = iota_bf(256)
     it16 = iota_bf(16)
     one = jnp.ones((256, 128), BF)
@@ -139,7 +127,7 @@
 def step_kernel(gas_hbm, cell_hbm, dest_hbm, slot_hbm, state_hbm, counts_hbm,
                 gas_out, state_out, arr_out,
                 g0, g1, t2, hy0, hy1, sy0, sy1, cell, dest, slot, state, counts,
-                tab, seen, rec, acc, rel, box, got,
+                tab, seen, leaver, stay, acc, rel, box, got,
                 in_sem, fars, farr, xs, xr, ys, yr, fs, fr):
     p, c = lax.axis_index("prop"), lax.axis_index("cross")
     np_, nc = lax.axis_size("prop"), lax.axis_size("cross")
@@ -236,7 +224,7 @@
         pltpu.make_async_copy(gas_hbm.at[pl.ds(3, 1)], g0.at[pl.ds(3, 1), pl.ds(1, 4)], in_sem.at[0]),
         pltpu.make_async_copy(gas_hbm.at[pl.ds(0, 3)], g0.at[pl.ds(0, 3), pl.ds(1, 4)], in_sem.at[1]),
         pltpu.make_async_copy(gas_hbm.at[pl.ds(4, 1)], g0.at[pl.ds(4, 1), pl.ds(1, 4)], in_sem.at[2]),
-        pltpu.make_async_copy(cell_hbm, cell, in_sem.at[3]),
+        pltpu.make_async_copy(cell_hbm, cell.at[pl.ds(0, 128)], in_sem.at[3]),
         pltpu.make_async_copy(state_hbm, state, in_sem.at[4]),
         pltpu.make_async_copy(slot_hbm, slot, in_sem.at[5]),
         pltpu.make_async_copy(dest_hbm, dest, in_sem.at[6]),
@@ -293,6 +281,33 @@
     send_near(0, 2)
     acc[...] = jnp.zeros_like(acc)
     rel[...] = jnp.zeros_like(rel)
+    for load in loads[3:]:
+        load.wait()
+
+    def on_blocks(rows, todo):
+        def body(b, carry):
+            todo(b, pl.ds(pl.multiple_of(b * rows, 8), rows))
+            return carry
+        lax.fori_loop(0, 2, body, 0)
+
+    def compact(b, ds):
+        mass = state[pl.ds(pl.multiple_of(2 * ROWS * b, 8), ROWS, stride=2), :]
+        temper = state[pl.ds(pl.multiple_of(2 * ROWS * b, 8) + 1, ROWS, stride=2), :]
+        compact_block(b, ROWS, slot[ds, :], dest[ds, :], cell[ds, :], mass, temper, acc)
+    on_blocks(ROWS, compact)
+    turned = acc[...].T
+    for f in range(4):
+        head, tail = turned[32 * f:32 * f + 16, :], turned[32 * f + 16:32 * f + 32, :]
+        both = head + tail if f < 2 else head * 256.0 + tail
+        if f == 2:
+            cell[128:144, :] = both[:, :128].astype(jnp.int32)
+            cell[144:160, :] = both[:, 128:].astype(jnp.int32)
+        elif f < 2:
+            leaver[f, 0:16, :] = both[:, :128]
+            leaver[f, 16:32, :] = both[:, 128:]
+        else:
+            box[0, 3] = both[:8]
+            box[1, 3] = both[8:]
 
     receive_near(0, 0)
     on_rest(lambda i: first(3, i))
@@ -312,8 +327,6 @@
     on_rest(winds)
     receive_near(0, 2)
     on_rest(lambda i: first(4, i))
-    for load in loads[3:]:
-        load.wait()
 
     def second_heat(half):
         def body(n, carry):
@@ -323,18 +336,12 @@
         lax.fori_loop(0, 2, body, 0)
         table(t2[pl.ds(2 * half, 2)].reshape(64, 512), tab)
 
-    def on_blocks(todo):
-        def body(b, carry):
-            todo(b, pl.ds(pl.multiple_of(b * ROWS, 8), ROWS))
-            return carry
-        lax.fori_loop(0, 128 // ROWS, body, 0)
-
     receive_near(1, 0)
     second_heat(near_half)
 
     def near_gather(b, ds):
         seen[ds, :] = gather_block(cell[ds, :], near_half, tab)
-    on_blocks(near_gather)
+    on_blocks(80, near_gather)
 
     receive_far(0, 0, 1, 2)
     winds(outer)
@@ -347,32 +354,35 @@
 
     def far_gather(b, ds):
         seen[ds, :] += gather_block(cell[ds, :], far_half, tab)
-    on_blocks(far_gather)
+    on_blocks(80, far_gather)
+    left_over, warm, burned = burn(leaver[0], leaver[1], seen[128:160, :])
+    place = lax.broadcasted_iota(jnp.int32, (8, 128), 0) * 256 + lax.broadcasted_iota(jnp.int32, (8, 128), 1)
+    for face in range(2):
+        for part in range(2):
+            lanes = slice(128 * part, 128 * part + 128)
+            live = place + 128 * part < counts[0, face]
+            at = 16 * part + 8 * face
+            for f, v in enumerate((left_over, warm, burned)):
+                box[face, f, :, lanes] = jnp.where(live, v[at:at + 8], 0.0)
+            box[face, 3, :, lanes] = jnp.where(live, box[face, 3, :, lanes], 0.0)
+    down = remote(box.at[0], got.at[1], fs.at[0], fr.at[0], below)
+    up = remote(box.at[1], got.at[0], fs.at[1], fr.at[1], above)
+    pl.when(has_below)(down.start)
+    pl.when(has_above)(up.start)
     receive_far(0, 4)
     first(4, outer)
     stage(1, 2)
     send_y(1, 2)
     send_far(1, 4)
     send_near(1, 2)
-    burn_all(state, seen[...], state_out, rec)
-    on_blocks(lambda b, ds: compact_block(b, ROWS, slot, dest, rec, acc))
-    place = lax.broadcasted_iota(jnp.int32, (8, 256), 0) * 256 + lax.broadcasted_iota(jnp.int32, (8, 256), 1)
-    turned = acc[...].T
-    for f in range(4):
-        head, tail = turned[32 * f:32 * f + 16, :], turned[32 * f + 16:32 * f + 32, :]
-        both = head * 256.0 + tail if f == 3 else head + tail
-        for face in range(2):
-            live = place < counts[0, face]
-            box[face, f] = jnp.where(live, both[8 * face:8 * face + 8], 0.0)
-    down = remote(box.at[0], got.at[1], fs.at[0], fr.at[0], below)
-    up = remote(box.at[1], got.at[0], fs.at[1], fr.at[1], above)
-    pl.when(has_below)(down.start)
-    pl.when(has_above)(up.start)
+    left_over, warm, burned = burn(state[pl.ds(0, 128, stride=2), :], state[pl.ds(1, 128, stride=2), :], seen[0:128, :])
+    state_out[pl.ds(0, 128, stride=2), :] = left_over
+    state_out[pl.ds(1, 128, stride=2), :] = warm
+    stay[...] = jnp.where(slot[...] < 0, burned, 0.0)
 
     def deposit(b, ds):
-        burned = jnp.where(slot[ds, :] < 0, rec[2, ds, :], 0.0)
-        deposit_block(dest[ds, :], burned, ROWS, rel)
-    on_blocks(deposit)
+        deposit_block(dest[ds, :], stay[ds, :], ROWS, rel)
+    on_blocks(ROWS, deposit)
 
     receive_near(1, 1)
 
@@ -419,6 +429,15 @@
                     halo_y(r, k, d).wait_send()
     pl.when(has_below)(down.wait_send)
     pl.when(has_above)(up.wait_send)
+
+
+def write_kernel(gas, state, arr, gas_hbm, state_hbm, arr_hbm, sem):
+    copies = [pltpu.make_async_copy(gas.at[f], gas_hbm.at[f], sem.at[f]) for f in range(5)]
+    copies += [pltpu.make_async_copy(state, state_hbm, sem.at[5]), pltpu.make_async_copy(arr, arr_hbm, sem.at[6])]
+    for copy in copies:
+        copy.start()
+    for copy in copies:
+        copy.wait()
 
 
 def on_device(gas, parcel_state, parcel_cell, parcel_dest, send_slot, face_counts):
@@ -442,14 +461,23 @@
         scratch_shapes=[
             f32(5, 6, 32, 512), f32(5, 6, 32, 512), f32(4, 32, 512),
             f32(5, 2, 4, 512), f32(5, 2, 4, 512), f32(5, 2, 4, 512), f32(5, 2, 4, 512),
-            i32(128, 128), i32(128, 128), i32(128, 128), f32(256, 128), pltpu.SMEM((1, 2), jnp.int32),
-            pltpu.VMEM((256, 256), BF), f32(128, 128), f32(3, 128, 128), f32(256, 128), f32(512, 256),
+            i32(160, 128), i32(128, 128), i32(128, 128), f32(256, 128), pltpu.SMEM((1, 2), jnp.int32),
+            pltpu.VMEM((256, 256), BF), f32(160, 128), f32(2, 32, 128), f32(128, 128), f32(256, 128), f32(512, 256),
             f32(2, 4, 8, 256), f32(2, 4, 8, 256),
             dma((8,)), dma((2, 5)), dma((2, 5)), dma((2, 3)), dma((2, 3)), dma((2, 3, 2)), dma((2, 3, 2)), dma((2,)), dma((2,)),
         ],
         compiler_params=pltpu.CompilerParams(vmem_limit_bytes=44 << 20, collective_id=0, has_side_effects=True),
         name="dust_step",
     )(*[pltpu.with_memory_space_constraint(a, pltpu.HBM) for a in inputs])
+    results = (gas_out, out, arr)
+    gas_out, out, arr = pl.pallas_call(
+        write_kernel,
+        out_shape=tuple(jax.ShapeDtypeStruct(a.shape, F32) for a in results),
+        in_specs=[vm] * 3,
+        out_specs=(hbm, hbm, hbm),
+        scratch_shapes=[dma((7,))],
+        name="write",
+    )(*[pltpu.with_memory_space_constraint(a, pltpu.VMEM) for a in results])
     parcels_out = out.reshape(128, 2, 128).transpose(1, 0, 2).reshape(2, 16384)
     arrivals = arr.reshape(3, 16, 2, 128).transpose(2, 0, 1, 3).reshape(2, 3, 2048)
     return (gas_out, parcels_out, arrivals)

time: 32.8 us -> 30.4 us (0.927)
  the two profiles are of different devices: /device:TPU:99 before, /device:TPU:7 now
where the time goes in v5:
time: 30.4 us; the launch traced here: 30.3 us
  Pallas kernels  29.7 us (98%)
  between operations  0.64 us (2%)
    pallas_call x1, Pallas kernels, on_device(): pl.pallas_call(step_kernel, out_shape=(jax.ShapeDtypeStruct(gas.shape, F3...  28.5 us
    pallas_call x1, Pallas kernels, on_device(): pl.pallas_call(write_kernel, out_shape=tuple((jax.ShapeDtypeStruct(a.shap...  1.16 us

profile of v5, /device:TPU:7, one launch (start us, length us, event | category | flops | bytes accessed | tf_op | source)
XLA Modules:
  0.0 30.3 jit_solution(17072465025159737160)
XLA Ops:
  0.6 28.5 %dust_step.1 = (f32[5,4,32,512]{3,2,1,0:T(8,128)S(1)}, f32[256,128]{1,0:T(8,128)S(1)}, f32[3,32,128]{2,1,0:T(8,128)S(1)}) custom-call(f32[5,4,32,512]{3,2,1,0:T(8,128)} %gas_hbm.1, s32[128,128]{1,0:T(8,128)} %bitcast.20, s32[128,128]{1,0:T(8,128)} %bitcast.21, s32[128,128]{1,0:T(8,128)} %bitcast.22, f32[256,128]{1,0:T(8,128)} %bitcast.19, s32[1,2]{1,0:T(1,128)} %bitcast.23), custom_call_target="tpu_custom_call" | custom-call | tf_op jit(solution)/shard_map/dust_step/pallas_call | solution.py:452
  29.2 1.2 %write.1 = (f32[5,4,32,512]{3,2,1,0:T(8,128)}, f32[256,128]{1,0:T(8,128)}, f32[3,32,128]{2,1,0:T(8,128)}) custom-call(f32[5,4,32,512]{3,2,1,0:T(8,128)S(1)} %get-tuple-element.9.gas, f32[256,128]{1,0:T(8,128)S(1)} %get-tuple-element.10.state, f32[3,32,128]{2,1,0:T(8,128)S(1)} %get-tuple-element.11.arr), custom_call_target="tpu_custom_call" | custom-call | tf_op jit(solution)/shard_map/write/pallas_call | solution.py:473

commit v6 on v5

--- a/solution.py
+++ b/solution.py
@@ -90,7 +90,7 @@
     acc_ref[...] += lax.dot_general(B, A, NT, preferred_element_type=F32)
 
 
-def deposit_block(dest, burned, rows, acc_ref):
+def deposit_block(dest, burned, rows):
     hi = key_of(dest)
     lo = low_of(dest)
     bh, bl = split(burned)
@@ -104,7 +104,7 @@
         As.append(jnp.concatenate([jnp.where(m, wide(bh[i:i + 1], 256), zero), jnp.where(m, wide(bl[i:i + 1], 256), zero)], axis=0))
     A = jnp.concatenate(As, axis=1)
     B = jnp.concatenate(Bs, axis=1)
-    acc_ref[...] += lax.dot_general(A, B, NT, preferred_element_type=F32)
+    return lax.dot_general(A, B, NT, preferred_element_type=F32)
 
 
 def plane(g, hy, f, i):
@@ -114,8 +114,8 @@
     lane = lax.broadcasted_iota(jnp.int32, (rows, 128), 1)
     xm, xp = g[f, i - 1], g[f, i + 1]
     down, up = pltpu.roll(c, 1, 0), pltpu.roll(c, rows - 1, 0)
-    ym = jnp.concatenate([jnp.where(row == 0, hy[f, 0, pl.ds(i - 1, 1), :], down[:8]), down[8:]], axis=0)
-    yp = jnp.concatenate([up[:-8], jnp.where(row == 7, hy[f, 1, pl.ds(i - 1, 1), :], up[-8:])], axis=0)
+    ym = jnp.concatenate([jnp.where(row == 0, hy[f, 0, i - 1], down[:8]), down[8:]], axis=0)
+    yp = jnp.concatenate([up[:-8], jnp.where(row == 7, hy[f, 1, i - 1], up[-8:])], axis=0)
     back, on = pltpu.roll(c, 1, 1), pltpu.roll(c, depth - 1, 1)
     zm = jnp.concatenate([jnp.where(lane == 0, 0.0, back[:, :128]), back[:, 128:]], axis=1)
     zp = jnp.concatenate([on[:, :-128], jnp.where(lane == 127, 0.0, on[:, -128:])], axis=1)
@@ -125,10 +125,10 @@
 
 
 def step_kernel(gas_hbm, cell_hbm, dest_hbm, slot_hbm, state_hbm, counts_hbm,
-                gas_out, state_out, arr_out,
+                gas_out, state_out, arr_out, come, rel,
                 g0, g1, t2, hy0, hy1, sy0, sy1, cell, dest, slot, state, counts,
-                tab, seen, leaver, stay, acc, rel, box, got,
-                in_sem, fars, farr, xs, xr, ys, yr, fs, fr):
+                tab, seen, leaver, stay, acc, box, got,
+                in_sem, fars, farr, xs, xr, ys, yr, hs, hr, fs, fr):
     p, c = lax.axis_index("prop"), lax.axis_index("cross")
     np_, nc = lax.axis_size("prop"), lax.axis_size("cross")
     side = lax.rem(p, 2)
@@ -163,11 +163,29 @@
         fields = pl.ds(lo, hi - lo)
         return remote(sys_[r].at[fields, d], hys[r].at[fields, 1 - d], ys.at[r, k, d], yr.at[r, k, d], right if d else left)
 
+    def heat_y(n, d):
+        planes = pl.ds(2 * (far_half if n else near_half), 2)
+        return remote(sy1.at[3, d, planes], hy1.at[3, 1 - d, planes], hs.at[n, d], hr.at[n, d], right if d else left)
+
+    def stage_heat(half):
+        for n in range(2):
+            i = 2 * half + n
+            sy1[3, 0, i] = g1[3, 1 + i, 0:1, :]
+            sy1[3, 1, i] = g1[3, 1 + i, 31:32, :]
+
+    def send_heat_y(n):
+        pl.when(has_left)(lambda: heat_y(n, 0).start())
+        pl.when(has_right)(lambda: heat_y(n, 1).start())
+
+    def receive_heat_y(n):
+        pl.when(has_left)(lambda: heat_y(n, 1).wait_recv())
+        pl.when(has_right)(lambda: heat_y(n, 0).wait_recv())
+
     def stage(r, k):
         for f in range(*GROUPS[k]):
             for i in range(4):
-                sys_[r][f, 0, i:i + 1, :] = gs[r][f, 1 + i, 0:1, :]
-                sys_[r][f, 1, i:i + 1, :] = gs[r][f, 1 + i, 31:32, :]
+                sys_[r][f, 0, i] = gs[r][f, 1 + i, 0:1, :]
+                sys_[r][f, 1, i] = gs[r][f, 1 + i, 31:32, :]
 
     def send_far(r, *fields):
         @pl.when(has_far)
@@ -215,10 +233,8 @@
         gas_out[f, i - 1] = fresh + 0.1 * g1[3, i] if f == 2 else fresh
 
     def on_rest(todo):
-        def body(n, carry):
+        for n in range(3):
             todo(rest + n)
-            return carry
-        lax.fori_loop(0, 3, body, 0)
 
     loads = [
         pltpu.make_async_copy(gas_hbm.at[pl.ds(3, 1)], g0.at[pl.ds(3, 1), pl.ds(1, 4)], in_sem.at[0]),
@@ -250,12 +266,12 @@
     @pl.when(c == 0)
     def _():
         for hy in hys:
-            hy[:, 0] = jnp.zeros((5, 4, 512), F32)
+            hy[:, 0] = jnp.zeros((5, 4, 1, 512), F32)
 
     @pl.when(c == nc - 1)
     def _():
         for hy in hys:
-            hy[:, 1] = jnp.zeros((5, 4, 512), F32)
+            hy[:, 1] = jnp.zeros((5, 4, 1, 512), F32)
 
     @pl.when(p == 0)
     def _():
@@ -288,7 +304,7 @@
         def body(b, carry):
             todo(b, pl.ds(pl.multiple_of(b * rows, 8), rows))
             return carry
-        lax.fori_loop(0, 2, body, 0)
+        lax.fori_loop(0, (160 if rows == 160 else 128) // rows, body, 0)
 
     def compact(b, ds):
         mass = state[pl.ds(pl.multiple_of(2 * ROWS * b, 8), ROWS, stride=2), :]
@@ -311,37 +327,38 @@
 
     receive_near(0, 0)
     on_rest(lambda i: first(3, i))
-    receive_far(0, 3)
-    first(3, outer)
-    stage(1, 0)
-    send_y(1, 0)
+    stage_heat(near_half)
+    send_heat_y(0)
     send_near(1, 0)
     send_far(0, 2)
-    send_far(1, 3)
-    send_far(0, 4)
     receive_near(0, 1)
 
     def winds(i):
         for f in range(3):
             first(f, i)
     on_rest(winds)
+    receive_far(0, 3)
+    first(3, outer)
+    stage_heat(far_half)
+    send_heat_y(1)
+    send_far(1, 3)
+    send_far(0, 4)
     receive_near(0, 2)
     on_rest(lambda i: first(4, i))
 
     def second_heat(half):
-        def body(n, carry):
+        for n in range(2):
             i = n + 2 * half
             t2[i] = plane(g1, hy1, 3, i + 1)
-            return carry
-        lax.fori_loop(0, 2, body, 0)
         table(t2[pl.ds(2 * half, 2)].reshape(64, 512), tab)
 
-    receive_near(1, 0)
+    halo_near(1, 0).wait_recv()
+    receive_heat_y(0)
     second_heat(near_half)
 
     def near_gather(b, ds):
         seen[ds, :] = gather_block(cell[ds, :], near_half, tab)
-    on_blocks(80, near_gather)
+    on_blocks(160, near_gather)
 
     receive_far(0, 0, 1, 2)
     winds(outer)
@@ -349,12 +366,13 @@
     send_y(1, 1)
     send_far(1, 0, 1, 2)
     send_near(1, 1)
+    receive_heat_y(1)
     receive_far(1, 3)
     second_heat(far_half)
 
     def far_gather(b, ds):
         seen[ds, :] += gather_block(cell[ds, :], far_half, tab)
-    on_blocks(80, far_gather)
+    on_blocks(160, far_gather)
     left_over, warm, burned = burn(leaver[0], leaver[1], seen[128:160, :])
     place = lax.broadcasted_iota(jnp.int32, (8, 128), 0) * 256 + lax.broadcasted_iota(jnp.int32, (8, 128), 1)
     for face in range(2):
@@ -381,15 +399,14 @@
     stay[...] = jnp.where(slot[...] < 0, burned, 0.0)
 
     def deposit(b, ds):
-        deposit_block(dest[ds, :], stay[ds, :], ROWS, rel)
+        rel[...] += deposit_block(dest[ds, :], stay[ds, :], ROWS)
+        for n in range(3):
+            gas_out[b, rest + n - 1] = plane(g1, hy1, b, rest + n)
+    receive_near(1, 1)
     on_blocks(ROWS, deposit)
 
-    receive_near(1, 1)
-
-    def later_winds(i):
-        for f in range(3):
-            second(f, i)
-    on_rest(later_winds)
+
+    on_rest(lambda i: second(2, i))
     receive_near(1, 2)
     on_rest(lambda i: second(4, i))
     for f in (0, 1, 2, 4):
@@ -398,19 +415,15 @@
 
     pl.when(has_below)(up.wait_recv)
     pl.when(has_above)(down.wait_recv)
-    where_to, burned = [], []
     for d in range(2):
         for part in range(2):
             lanes = slice(128 * part, 128 * part + 128)
-            where_to.append(got[d, 3, :, lanes].astype(jnp.int32))
-            burned.append(got[d, 2, :, lanes])
+            at = 16 * d + 8 * part
+            come[0, at:at + 8, :] = got[d, 2, :, lanes]
+            come[1, at:at + 8, :] = got[d, 3, :, lanes]
             for f in range(3):
                 arr_out[f, pl.ds(2 * part + d, 8, stride=4), :] = got[d, f, :, lanes]
-    deposit_block(jnp.concatenate(where_to, axis=0), jnp.concatenate(burned, axis=0), 32, rel)
-    both = rel[:256, :] + rel[256:, :]
-    release = jnp.concatenate([both[:128], both[128:]], axis=1).reshape(4, 32, 512)
-    gas_out[3] = t2[...] + 1.5 * release
-    gas_out[4] = gas_out[4] + release
+    gas_out[3] = t2[...]
 
     @pl.when(has_far)
     def _():
@@ -425,17 +438,25 @@
         @pl.when(there)
         def _():
             for r in range(2):
-                for k in range(3):
+                for k in range(r, 3):
                     halo_y(r, k, d).wait_send()
+                heat_y(r, d).wait_send()
     pl.when(has_below)(down.wait_send)
     pl.when(has_above)(up.wait_send)
 
 
-def write_kernel(gas, state, arr, gas_hbm, state_hbm, arr_hbm, sem):
-    copies = [pltpu.make_async_copy(gas.at[f], gas_hbm.at[f], sem.at[f]) for f in range(5)]
+def write_kernel(gas, state, arr, come, rel, gas_hbm, state_hbm, arr_hbm, last, sem):
+    copies = [pltpu.make_async_copy(gas.at[f], gas_hbm.at[f], sem.at[f]) for f in range(3)]
     copies += [pltpu.make_async_copy(state, state_hbm, sem.at[5]), pltpu.make_async_copy(arr, arr_hbm, sem.at[6])]
     for copy in copies:
         copy.start()
+    release = rel[...] + deposit_block(come[1].astype(jnp.int32), come[0], 32)
+    both = release[:256, :] + release[256:, :]
+    release = jnp.concatenate([both[:128], both[128:]], axis=1).reshape(4, 32, 512)
+    for n in range(2):
+        last[n] = gas[3 + n] + (1.5 * release if n == 0 else release)
+        copies.append(pltpu.make_async_copy(last.at[n], gas_hbm.at[3 + n], sem.at[3 + n]))
+        copies[-1].start()
     for copy in copies:
         copy.wait()
 
@@ -449,33 +470,35 @@
     f32 = lambda *s: pltpu.VMEM(s, F32)
     dma = pltpu.SemaphoreType.DMA
     inputs = (gas, square(parcel_cell), square(parcel_dest), square(send_slot), state, face_counts.reshape(1, 2))
-    gas_out, out, arr = pl.pallas_call(
+    results = pl.pallas_call(
         step_kernel,
         out_shape=(
             jax.ShapeDtypeStruct(gas.shape, F32),
             jax.ShapeDtypeStruct((256, 128), F32),
             jax.ShapeDtypeStruct((3, 32, 128), F32),
+            jax.ShapeDtypeStruct((2, 32, 128), F32),
+            jax.ShapeDtypeStruct((512, 256), F32),
         ),
         in_specs=[hbm] * 6,
-        out_specs=(vm, vm, vm),
+        out_specs=(vm,) * 5,
         scratch_shapes=[
             f32(5, 6, 32, 512), f32(5, 6, 32, 512), f32(4, 32, 512),
-            f32(5, 2, 4, 512), f32(5, 2, 4, 512), f32(5, 2, 4, 512), f32(5, 2, 4, 512),
+            f32(5, 2, 4, 1, 512), f32(5, 2, 4, 1, 512), f32(5, 2, 4, 1, 512), f32(5, 2, 4, 1, 512),
             i32(160, 128), i32(128, 128), i32(128, 128), f32(256, 128), pltpu.SMEM((1, 2), jnp.int32),
-            pltpu.VMEM((256, 256), BF), f32(160, 128), f32(2, 32, 128), f32(128, 128), f32(256, 128), f32(512, 256),
+            pltpu.VMEM((256, 256), BF), f32(160, 128), f32(2, 32, 128), f32(128, 128), f32(256, 128),
             f32(2, 4, 8, 256), f32(2, 4, 8, 256),
-            dma((8,)), dma((2, 5)), dma((2, 5)), dma((2, 3)), dma((2, 3)), dma((2, 3, 2)), dma((2, 3, 2)), dma((2,)), dma((2,)),
+            dma((8,)), dma((2, 5)), dma((2, 5)), dma((2, 3)), dma((2, 3)), dma((2, 3, 2)), dma((2, 3, 2)), dma((2, 2)), dma((2, 2)), dma((2,)), dma((2,)),
         ],
         compiler_params=pltpu.CompilerParams(vmem_limit_bytes=44 << 20, collective_id=0, has_side_effects=True),
         name="dust_step",
     )(*[pltpu.with_memory_space_constraint(a, pltpu.HBM) for a in inputs])
-    results = (gas_out, out, arr)
     gas_out, out, arr = pl.pallas_call(
         write_kernel,
-        out_shape=tuple(jax.ShapeDtypeStruct(a.shape, F32) for a in results),
-        in_specs=[vm] * 3,
+        out_shape=tuple(jax.ShapeDtypeStruct(a.shape, F32) for a in results[:3]),
+        in_specs=[vm] * 5,
         out_specs=(hbm, hbm, hbm),
-        scratch_shapes=[dma((7,))],
+        scratch_shapes=[f32(2, 4, 32, 512), dma((7,))],
+        compiler_params=pltpu.CompilerParams(vmem_limit_bytes=16 << 20),
         name="write",
     )(*[pltpu.with_memory_space_constraint(a, pltpu.VMEM) for a in results])
     parcels_out = out.reshape(128, 2, 128).transpose(1, 0, 2).reshape(2, 16384)

time: 30.4 us -> 29.9 us (0.984)
  Pallas kernels: 29.7 us -> 29.2 us
    pallas_call x1, Pallas kernels: 28.5 us -> 27 us  [on_device(): pl.pallas_call(step_kernel, out_shape=(jax.ShapeDtypeStruct(gas.shape, F3...]
    pallas_call x1, Pallas kernels: 1.16 us -> 2.14 us  [on_device(): pl.pallas_call(write_kernel, out_shape=tuple((jax.ShapeDtypeStruct(a.shap...]
where the time goes in v6:
time: 29.9 us; the launch traced here: 29.8 us
  Pallas kernels  29.2 us (98%)
  between operations  0.64 us (2%)
    pallas_call x1, Pallas kernels, on_device(): pl.pallas_call(step_kernel, out_shape=(jax.ShapeDtypeStruct(gas.shape, F3...  27 us
    pallas_call x1, Pallas kernels, on_device(): pl.pallas_call(write_kernel, out_shape=tuple((jax.ShapeDtypeStruct(a.shap...  2.14 us

profile of v6, /device:TPU:7, one launch (start us, length us, event | category | flops | bytes accessed | tf_op | source)
XLA Modules:
  0.0 29.8 jit_solution(13026316881888901136)
XLA Ops:
  0.6 27.0 %dust_step.1 = (f32[5,4,32,512]{3,2,1,0:T(8,128)S(1)}, f32[256,128]{1,0:T(8,128)S(1)}, f32[3,32,128]{2,1,0:T(8,128)S(1)}, f32[2,32,128]{2,1,0:T(8,128)S(1)}, f32[512,256]{1,0:T(8,128)S(1)}) custom-call(f32[5,4,32,512]{3,2,1,0:T(8,128)} %gas_hbm.1, s32[128,128]{1,0:T(8,128)} %bitcast.20, s32[128,128]{1,0:T(8,128)} %bitcast.21, s32[128,128]{1,0:T(8,128)} %bitcast.22, ...), custom_call_target="tpu_custom_call" | custom-call | tf_op jit(solution)/shard_map/dust_step/pallas_call | solution.py:473
  27.7 2.1 %write.1 = (f32[5,4,32,512]{3,2,1,0:T(8,128)}, f32[256,128]{1,0:T(8,128)}, f32[3,32,128]{2,1,0:T(8,128)}) custom-call(f32[5,4,32,512]{3,2,1,0:T(8,128)S(1)} %get-tuple-element.11.gas, f32[256,128]{1,0:T(8,128)S(1)} %get-tuple-element.12.state, f32[3,32,128]{2,1,0:T(8,128)S(1)} %get-tuple-element.13.arr, f32[2,32,128]{2,1,0:T(8,128)S(1)} %get-tuple-element.14.come, ...), custom_call_target="tpu_custom_call" | custom-call | tf_op jit(solution)/shard_map/write/pallas_call | solution.py:495

commit v7 on v6

--- a/solution.py
+++ b/solution.py
@@ -292,7 +292,7 @@
     send_far(0, 3)
     send_near(0, 0)
     send_y(0, 1, 2)
-    send_far(0, 0, 1)
+    send_far(0, 0)
     send_near(0, 1)
     send_near(0, 2)
     acc[...] = jnp.zeros_like(acc)
@@ -330,7 +330,7 @@
     stage_heat(near_half)
     send_heat_y(0)
     send_near(1, 0)
-    send_far(0, 2)
+    send_far(0, 1, 2)
     receive_near(0, 1)
 
     def winds(i):

time: 29.9 us -> 28.4 us (0.950)
  Pallas kernels: 29.2 us -> 27.6 us
    pallas_call x1, Pallas kernels: 27 us -> 25.5 us  [on_device(): pl.pallas_call(step_kernel, out_shape=(jax.ShapeDtypeStruct(gas.shape, F3...]
where the time goes in v7:
time: 28.4 us; the launch traced here: 28.3 us
  Pallas kernels  27.6 us (97%)
  between operations  0.64 us (2%)
    pallas_call x1, Pallas kernels, on_device(): pl.pallas_call(step_kernel, out_shape=(jax.ShapeDtypeStruct(gas.shape, F3...  25.5 us
    pallas_call x1, Pallas kernels, on_device(): pl.pallas_call(write_kernel, out_shape=tuple((jax.ShapeDtypeStruct(a.shap...  2.15 us

profile of v7, /device:TPU:7, one launch (start us, length us, event | category | flops | bytes accessed | tf_op | source)
XLA Modules:
  0.0 28.3 jit_solution(1914758462750543164)
XLA Ops:
  0.6 25.5 %dust_step.1 = (f32[5,4,32,512]{3,2,1,0:T(8,128)S(1)}, f32[256,128]{1,0:T(8,128)S(1)}, f32[3,32,128]{2,1,0:T(8,128)S(1)}, f32[2,32,128]{2,1,0:T(8,128)S(1)}, f32[512,256]{1,0:T(8,128)S(1)}) custom-call(f32[5,4,32,512]{3,2,1,0:T(8,128)} %gas_hbm.1, s32[128,128]{1,0:T(8,128)} %bitcast.20, s32[128,128]{1,0:T(8,128)} %bitcast.21, s32[128,128]{1,0:T(8,128)} %bitcast.22, ...), custom_call_target="tpu_custom_call" | custom-call | tf_op jit(solution)/shard_map/dust_step/pallas_call | solution.py:473
  26.1 2.1 %write.1 = (f32[5,4,32,512]{3,2,1,0:T(8,128)}, f32[256,128]{1,0:T(8,128)}, f32[3,32,128]{2,1,0:T(8,128)}) custom-call(f32[5,4,32,512]{3,2,1,0:T(8,128)S(1)} %get-tuple-element.11.gas, f32[256,128]{1,0:T(8,128)S(1)} %get-tuple-element.12.state, f32[3,32,128]{2,1,0:T(8,128)S(1)} %get-tuple-element.13.arr, f32[2,32,128]{2,1,0:T(8,128)S(1)} %get-tuple-element.14.come, ...), custom_call_target="tpu_custom_call" | custom-call | tf_op jit(solution)/shard_map/write/pallas_call | solution.py:495

commit v8 on v7

--- a/solution.py
+++ b/solution.py
@@ -326,11 +326,13 @@
             box[1, 3] = both[8:]
 
     receive_near(0, 0)
-    on_rest(lambda i: first(3, i))
+    first(3, 1 + 2 * near_half)
+    first(3, 2 + 2 * near_half)
     stage_heat(near_half)
     send_heat_y(0)
     send_near(1, 0)
     send_far(0, 1, 2)
+    first(3, 2 + side)
     receive_near(0, 1)
 
     def winds(i):
@@ -399,11 +401,12 @@
     stay[...] = jnp.where(slot[...] < 0, burned, 0.0)
 
     def deposit(b, ds):
-        rel[...] += deposit_block(dest[ds, :], stay[ds, :], ROWS)
-        for n in range(3):
-            gas_out[b, rest + n - 1] = plane(g1, hy1, b, rest + n)
+        rel[...] += deposit_block(dest[ds, :], stay[ds, :], 128)
+        for f in range(2):
+            for n in range(3):
+                gas_out[f, rest + n - 1] = plane(g1, hy1, f, rest + n)
     receive_near(1, 1)
-    on_blocks(ROWS, deposit)
+    on_blocks(128, deposit)
 
 
     on_rest(lambda i: second(2, i))

time: 28.4 us -> 28.3 us (level)
  no operation moved by 1% of the time
where the time goes in v8:
time: 28.3 us; the launch traced here: 28.1 us
  Pallas kernels  27.5 us (97%)
  between operations  0.64 us (2%)
    pallas_call x1, Pallas kernels, on_device(): pl.pallas_call(step_kernel, out_shape=(jax.ShapeDtypeStruct(gas.shape, F3...  25.3 us
    pallas_call x1, Pallas kernels, on_device(): pl.pallas_call(write_kernel, out_shape=tuple((jax.ShapeDtypeStruct(a.shap...  2.16 us

profile of v8, /device:TPU:7, one launch (start us, length us, event | category | flops | bytes accessed | tf_op | source)
XLA Modules:
  0.0 28.1 jit_solution(8391968589033870498)
XLA Ops:
  0.6 25.3 %dust_step.1 = (f32[5,4,32,512]{3,2,1,0:T(8,128)S(1)}, f32[256,128]{1,0:T(8,128)S(1)}, f32[3,32,128]{2,1,0:T(8,128)S(1)}, f32[2,32,128]{2,1,0:T(8,128)S(1)}, f32[512,256]{1,0:T(8,128)S(1)}) custom-call(f32[5,4,32,512]{3,2,1,0:T(8,128)} %gas_hbm.1, s32[128,128]{1,0:T(8,128)} %bitcast.20, s32[128,128]{1,0:T(8,128)} %bitcast.21, s32[128,128]{1,0:T(8,128)} %bitcast.22, ...), custom_call_target="tpu_custom_call" | custom-call | tf_op jit(solution)/shard_map/dust_step/pallas_call | solution.py:476
  26.0 2.2 %write.1 = (f32[5,4,32,512]{3,2,1,0:T(8,128)}, f32[256,128]{1,0:T(8,128)}, f32[3,32,128]{2,1,0:T(8,128)}) custom-call(f32[5,4,32,512]{3,2,1,0:T(8,128)S(1)} %get-tuple-element.11.gas, f32[256,128]{1,0:T(8,128)S(1)} %get-tuple-element.12.state, f32[3,32,128]{2,1,0:T(8,128)S(1)} %get-tuple-element.13.arr, f32[2,32,128]{2,1,0:T(8,128)S(1)} %get-tuple-element.14.come, ...), custom_call_target="tpu_custom_call" | custom-call | tf_op jit(solution)/shard_map/write/pallas_call | solution.py:498
